TPU v7x, 32 devices: a whole 2x2x4 slice. The times are simulated.
32 devices in a mesh: freq: 2 (over y), src: 8 (over z, x), rcv: 2 (over core).
Axes of the slice: x: 2, y: 2, z: 4, core: 2. Of those that a mesh axis runs over, the one named last changes fastest.
Arguments:
- panel: float32 [4, 1024, 5632], P('freq', 'src', 'rcv'), parts along dimension 0, may hold values from -6 to 6
- obliquity: float32 [4, 131072], P('freq'), parts along dimension 0, may hold values from -0.125 to 0.125
- panel_stations: int32 [1024], replicated, may hold values from 0 to 131071
- tile_map: int32 [512, 2], P('freq'), parts along dimension 0, may hold values from -1 to 21, as said below
- recorded: float32 [256, 4, 256, 256], P(('src', 'rcv'), 'freq'), parts along dimension 1, may hold values from -6 to 6
Outputs:
- demultiple: float32 [256, 4, 256, 256], P(('src', 'rcv'), 'freq'), parts along dimension 1
There are 2 independent parts, one for each index of `freq`. A program takes and returns all parts, laid end to end along the dimension named above; an argument that names none is the same for every part. Nothing has to cross between parts.
Inputs may be any that keep to these rules, and one draw needn't show every extreme that they name: `tile_map`: each slot holds a row tile i and a column tile j with j <= i; each of the 253 such tiles stands in exactly one slot; remaining slots hold -1 in both entries.
All inputs are finite; a program needn't handle non-finite values.
Results may differ from a plain program's by a relative error of at most 0.0044.
Values may be sent and summed in bfloat16 or wider, within the bound.
No kernel may reach another device: no remote copies, remote signals or barrier semaphores. Data moves between devices by JAX's collectives and lax.ppermute only.
A program may use at most 192 MiB of HBM per device.

v0:
```python
import jax
import jax.numpy as jnp
from jax import lax
from jax.sharding import PartitionSpec as P


def tile_products(weight_k, row_part, col_part):
    left = row_part[:, :, 0].astype(jnp.float32)
    w_real = weight_k[0][:, None, None]
    w_imag = weight_k[1][:, None, None]
    weighted = jnp.stack(
        [w_real * left[0] - w_imag * left[1], w_real * left[1] + w_imag * left[0]]
    ).astype(jnp.bfloat16)
    right = col_part[:, :, 0]
    form = "knr,knc->nrc"
    real_part = jnp.einsum(
        form, weighted[0], right[0], preferred_element_type=jnp.float32
    ) - jnp.einsum(form, weighted[1], right[1], preferred_element_type=jnp.float32)
    imag_part = jnp.einsum(
        form, weighted[0], right[1], preferred_element_type=jnp.float32
    ) + jnp.einsum(form, weighted[1], right[0], preferred_element_type=jnp.float32)
    return jnp.stack([real_part, imag_part], axis=1)


def body(panel, obliquity, panel_stations, tile_map, recorded):
    n_src = lax.axis_size("src")
    n_rcv = lax.axis_size("rcv")
    rcv_index = lax.axis_index("rcv")
    src_index = lax.axis_index("src")
    slots_dev = recorded.shape[0]
    tile_side = recorded.shape[2]
    local = panel.astype(jnp.bfloat16)
    full_rows = lax.all_gather(local, "rcv", axis=2, tiled=True)
    tiled = full_rows.reshape(2, full_rows.shape[1], full_rows.shape[2] // tile_side, tile_side)
    dest_dev = jnp.arange(n_src, dtype=jnp.int32) * n_rcv + rcv_index
    slot_ids = dest_dev[:, None] * slots_dev + jnp.arange(slots_dev, dtype=jnp.int32)[None, :]
    dest_rows = jnp.maximum(tile_map[slot_ids, 0], 0)
    dest_cols = jnp.maximum(tile_map[slot_ids, 1], 0)
    row_send = jnp.take(tiled, dest_rows, axis=2)
    col_send = jnp.take(tiled, dest_cols, axis=2)
    weight_k = jnp.take(obliquity, panel_stations, axis=1)
    row_recv = lax.all_to_all(row_send, "src", split_axis=2, concat_axis=1, tiled=True)
    col_recv = lax.all_to_all(col_send, "src", split_axis=2, concat_axis=1, tiled=True)
    predicted = tile_products(weight_k, row_recv, col_recv)
    own_dev = src_index * n_rcv + rcv_index
    own_slots = own_dev * slots_dev + jnp.arange(slots_dev, dtype=jnp.int32)
    valid = (tile_map[own_slots, 0] >= 0).astype(jnp.float32)
    return recorded - valid[:, None, None, None] * predicted


def solution(mesh):
    return jax.shard_map(
        body,
        mesh=mesh,
        in_specs=(
            P("freq", "src", "rcv"),
            P("freq", None),
            P(),
            P("freq", None),
            P(("src", "rcv"), "freq", None, None),
        ),
        out_specs=P(("src", "rcv"), "freq", None, None),
        check_vma=False,
    )
```

profile of v0, /device:TPU:0, one launch (start us, length us, event | category | flops | bytes accessed | tf_op | source)
XLA Modules:
  0.0 883.5 jit_solution(2225517150078380643)
XLA Ops:
  6.5 0.0 copy-start
  6.5 0.0 all-gather.2.cloned.1.call-start
  6.5 2.9 copy.13
  9.5 0.0 all-gather.2.cloned.1.call-update
  9.5 0.1 broadcast_or_fusion
  9.6 0.1 reshape.124
  9.7 1.5 gather_fusion.2
  11.2 0.1 reshape.142
  11.3 0.1 reshape.145
  11.4 12.7 %all-gather.2.cloned.1.call-done = bf16[2,128,5632]{1,2,0:T(8,128)(2,1)} async-done(((bf16[2,128,2816]{1,2,0:T(8,128)(2,1)}), bf16[2,128,5632]{1,2,0:T(8,128)(2,1)}) %all-gather.2.cloned.1.call-update) | async-done | bytes 2883600 | tf_op jit(solution)/shard_map/all_gather | solution.py:33
  24.1 3.1 copy.14
  27.2 8.3 gather_fusion.4
  35.5 14.2 %select_bitcast_fusion.1 = bf16[2,128,8,16,256]{4,1,0,3,2:T(8,128)(2,1)} fusion(bf16[8,16,2,128,256]{4,3,2,1,0:T(8,128)(2,1)} %bitcast.56, pred[8,16]{1,0:T(8,128)(4,1)S(1)} %compare_and_fusion.1), kind=kLoop, calls=%fused_computation.8 | loop fusion | flops 8388608 | bytes 33554560 | tf_op jit(solution)/shard_map/jit(_take)/select_n | solution.py:39
  49.7 5.8 all-to-all-start
  55.5 0.1 reshape.130
  55.6 1.5 gather_fusion.3
  57.1 0.1 reshape.144
  57.2 0.1 reshape.149
  57.3 8.3 gather_fusion.5
  65.6 14.2 %select_bitcast_fusion = bf16[2,128,8,16,256]{4,1,0,3,2:T(8,128)(2,1)} fusion(bf16[8,16,2,128,256]{4,3,2,1,0:T(8,128)(2,1)} %bitcast.55, pred[8,16]{1,0:T(8,128)(4,1)S(1)} %compare_and_fusion), kind=kLoop, calls=%fused_computation.7 | loop fusion | flops 8388608 | bytes 33554560 | tf_op jit(solution)/shard_map/jit(_take)/select_n | solution.py:40
  79.8 339.3 %all-to-all-done = bf16[2,128,8,16,256]{4,1,0,3,2:T(8,128)(2,1)} async-done(((bf16[2,128,8,16,256]{4,1,0,3,2:T(8,128)(2,1)}), bf16[2,128,8,16,256]{4,1,0,3,2:T(8,128)(2,1)}, u32[]{:S(2)}, u32[]{:S(2)}) %all-to-all-start) | async-done | bytes 16777248 | tf_op jit(solution)/shard_map/all_to_all | solution.py:42
  419.2 5.7 all-to-all-start.1
  424.9 0.0 copy-done.3
  424.9 0.0 copy-start.4
  424.9 29.9 %copy.12 = f32[2,131072]{0,1:T(8,128)} copy(f32[2,131072]{1,0:T(2,128)S(1)} %copy-done.3) | data formatting | bytes 2097152 | tf_op args[1]
  454.8 0.7 gather_fusion
  455.5 10.5 %gather_fusion.1 = f32[1024,2]{1,0:T(8,128)S(1)} fusion(f32[2,131072]{0,1:T(8,128)} %copy.12, s32[1024]{0:T(1024)S(1)} %fusion.5), kind=kCustom, calls=%fused_computation.3 | custom fusion | bytes 20480 | tf_op jit(solution)/shard_map/jit(_take)/gather | solution.py:41
  466.1 0.2 select_bitcast_fusion.2
  466.3 0.5 slice_reduce_fusion.1
  466.8 18.7 %convert_bitcast_fusion = f32[2,8,128,1,16,256]{5,2,0,4,1,3:T(8,128)} fusion(bf16[2,128,8,16,256]{4,1,0,3,2:T(8,128)(2,1)} %all-to-all-done), kind=kLoop, calls=%fused_computation.6 | loop fusion | flops 8388608 | bytes 50331648 | tf_op jit(solution)/shard_map/convert_element_type | solution.py:8
  485.5 21.4 %fusion.9 = (f32[1,8,128,1,16,256]{5,2,0,4,1,3:T(8,128)}, f32[1,8,128,1,16,256]{5,2,0,4,1,3:T(8,128)}) fusion(f32[2,8,128,1,16,256]{5,2,0,4,1,3:T(8,128)} %convert_bitcast_fusion), kind=kLoop, calls=%fused_computation.41 | loop fusion | bytes 67108864 | tf_op jit(solution)/shard_map/slice | solution.py:12
  506.9 17.8 %copy.15 = f32[1,8,128,1,16,256]{2,1,5,4,3,0:T(8,128)} copy(f32[1,8,128,1,16,256]{5,2,0,4,1,3:T(8,128)} %get-tuple-element.10) | data formatting | bytes 33554432 | tf_op jit(solution)/shard_map/slice | solution.py:12
  524.8 18.0 %slice.40 = f32[1,1024,16,256]{1,3,2,0:T(8,128)} reshape(f32[1,8,128,1,16,256]{2,1,5,4,3,0:T(8,128)} %copy.15) | data formatting | bytes 33554432 | tf_op jit(solution)/shard_map/slice | solution.py:12
  542.7 17.8 %copy.16 = f32[1,8,128,1,16,256]{2,1,5,4,3,0:T(8,128)} copy(f32[1,8,128,1,16,256]{5,2,0,4,1,3:T(8,128)} %get-tuple-element.11) | data formatting | bytes 33554432 | tf_op jit(solution)/shard_map/slice | solution.py:12
  560.6 18.0 %slice.43 = f32[1,1024,16,256]{1,3,2,0:T(8,128)} reshape(f32[1,8,128,1,16,256]{2,1,5,4,3,0:T(8,128)} %copy.16) | data formatting | bytes 33554432 | tf_op jit(solution)/shard_map/slice | solution.py:12
  578.6 209.0 %all-to-all-done.1 = bf16[2,128,8,16,256]{4,1,0,3,2:T(8,128)(2,1)} async-done(((bf16[2,128,8,16,256]{4,1,0,3,2:T(8,128)(2,1)}), bf16[2,128,8,16,256]{4,1,0,3,2:T(8,128)(2,1)}, u32[]{:S(2)}, u32[]{:S(2)}) %all-to-all-start.1) | async-done | bytes 16777248 | tf_op jit(solution)/shard_map/all_to_all | solution.py:43
  787.6 11.8 %fusion.10 = (bf16[1,8,128,1,16,256]{5,2,0,4,1,3:T(8,128)(2,1)}, bf16[1,8,128,1,16,256]{5,2,0,4,1,3:T(8,128)(2,1)}) fusion(bf16[2,8,128,1,16,256]{5,2,0,4,1,3:T(8,128)(2,1)} %bitcast.12), kind=kLoop, calls=%fused_computation.42 | loop fusion | bytes 33554432 | tf_op jit(solution)/shard_map/slice | solution.py:17
  799.4 7.7 copy.18
  807.1 7.8 copy.19
  815.0 17.5 %fusion.1 = (bf16[1024,16,256]{0,2,1:T(8,128)(2,1)}, bf16[1024,16,256]{0,2,1:T(8,128)(2,1)}) fusion(f32[1,1024,16,256]{1,3,2,0:T(8,128)} %slice.40, f32[1,1024,16,256]{1,3,2,0:T(8,128)} %slice.43, f32[1024]{0:T(1024)S(1)} %get-tuple-element.7, f32[1024]{0:T(1024)S(1)} %get-tuple-element.6), kind=kLoop, calls=%fused_computation.12 | loop fusion | flops 33554432 | bytes 50339840 | tf_op jit(solution)/shard_map/squeeze | solution.py:18
  832.4 0.0 slice-done
  832.5 0.0 copy-start.2
  832.5 7.9 fusion.11
  840.4 7.8 fusion.12
  848.2 9.0 %subtract_bitcast_fusion = f32[16,1,256,256]{3,2,0,1:T(8,128)} fusion(f32[16,256,256]{2,1,0:T(8,128)} %fusion.11, bf16[1024,16,256]{0,2,1:T(8,128)(2,1)} %get-tuple-element.8, bf16[1024,16,256]{2,0,1:T(8,128)(2,1)S(1)} %bitcast.54), kind=kOutput, calls=%fused_computation.16 | convolution fusion | flops 2148532224 | bytes 25165824 | tf_op jit(solution)/shard_map/knr,knc->nrc/dot_general | solution.py:18
  857.2 9.0 %add_bitcast_fusion = f32[16,1,256,256]{3,2,0,1:T(8,128)} fusion(f32[16,256,256]{2,1,0:T(8,128)} %fusion.12, bf16[1024,16,256]{0,2,1:T(8,128)(2,1)} %get-tuple-element.8, bf16[1024,16,256]{2,0,1:T(8,128)(2,1)S(1)} %bitcast.52), kind=kOutput, calls=%fused_computation.15 | convolution fusion | flops 2148532224 | bytes 25165824 | tf_op jit(solution)/shard_map/knr,knc->nrc/dot_general | solution.py:21
  866.2 6.5 fusion.2
  872.7 4.0 copy.21
  (23 shorter events, 0.1 us)
Async XLA Ops:
  6.5 3.1 copy-start
  6.5 17.6 %all-gather.2.cloned.1.call-start = ((), (), s32[]{:S(2)}) async-start(), calls=%async_computation.2 | async-start | bytes 4325376 | tf_op jit(solution)/shard_map/all_gather | solution.py:33
  49.7 369.4 %all-to-all-start = ((bf16[2,128,8,16,256]{4,1,0,3,2:T(8,128)(2,1)}), bf16[2,128,8,16,256]{4,1,0,3,2:T(8,128)(2,1)}, u32[]{:S(2)}, u32[]{:S(2)}) async-start(bf16[2,128,8,16,256]{4,1,0,3,2:T(8,128)(2,1)} %select_bitcast_fusion.1), calls=%async_computation | async-start | bytes 33554432 | tf_op jit(solution)/shard_map/all_to_all | solution.py:42
  79.8 345.1 %copy-start.3 = (f32[2,131072]{1,0:T(2,128)S(1)}, f32[2,131072]{1,0:T(2,128)}, u32[]{:S(2)}) copy-start(f32[2,131072]{1,0:T(2,128)} %param.8) | copy-start | bytes 3145732
  419.2 368.4 %all-to-all-start.1 = ((bf16[2,128,8,16,256]{4,1,0,3,2:T(8,128)(2,1)}), bf16[2,128,8,16,256]{4,1,0,3,2:T(8,128)(2,1)}, u32[]{:S(2)}, u32[]{:S(2)}) async-start(bf16[2,128,8,16,256]{4,1,0,3,2:T(8,128)(2,1)} %select_bitcast_fusion), calls=%async_computation.1 | async-start | bytes 33554432 | tf_op jit(solution)/shard_map/all_to_all | solution.py:43
  424.9 30.6 %copy-start.4 = (s32[1024]{0:T(1024)S(1)}, s32[1024]{0:T(1024)}, u32[]{:S(2)}) copy-start(s32[1024]{0:T(1024)} %param.9) | copy-start | bytes 12292
  807.1 25.3 %slice-start = ((s8[8388608]{0:T(1024)(128)(4,1)}), s8[4194304]{0:T(1024)(128)(4,1)S(1)}, s32[]{:S(2)}) async-start(s8[8388608]{0:T(1024)(128)(4,1)} %bitcast.49), calls=%async_computation.3 | async-start | bytes 8388608
  815.0 17.5 %slice-start.1 = ((s8[8388608]{0:T(1024)(128)(4,1)}), s8[4194304]{0:T(1024)(128)(4,1)S(1)}, s32[]{:S(2)}) async-start(s8[8388608]{0:T(1024)(128)(4,1)} %bitcast.49), calls=%async_computation.4 | async-start | bytes 8388608
  832.5 7.9 copy-start.2
  866.2 10.5 %copy-start.1 = (s32[256,2]{0,1:T(2,128)S(1)}, s32[256,2]{0,1:T(2,128)}, u32[]{:S(2)}) copy-start(s32[256,2]{0,1:T(2,128)} %param.10) | copy-start | bytes 6148
Sparse Core Ops, SparseCore 0:
  9.6 14.4 all-gather.1
where the time goes:
time: 886 us; the launch traced here: 884 us
  waiting for transfers between devices  561 us (63%)
  local copies, waits for them, and re-layouts  192 us (22%)
  other arithmetic  71.4 us (8%)
  matrix products  33.7 us (4%)
  between operations  13.6 us (2%)
  starting transfers between devices  11.5 us (1%)
    all_to_all x1, waiting for transfers between devices, body(): lax.all_to_all(row_send, 'src', split_axis=2, concat_axis=1, tiled=True)  339 us
    all_to_all x1, waiting for transfers between devices, body(): lax.all_to_all(col_send, 'src', split_axis=2, concat_axis=1, tiled=True)  209 us
    slice x3, local copies, waits for them, and re-layouts, tile_products(): left[0]  57.2 us
    slice x2, local copies, waits for them, and re-layouts, tile_products(): left[1]  35.8 us
    unnamed x16, local copies, waits for them, and re-layouts  32.9 us
    slice x2, local copies, waits for them, and re-layouts, tile_products(): right[0]  19.6 us
    convert_element_type x1, other arithmetic, tile_products(): left = row_part[:, :, 0].astype(jnp.float32)  18.7 us
  transfers between devices with their start and end apart: 3, of which 3 were waited for; matrix products, arithmetic and copies ran while one was open for 20% of the time, Pallas kernels for 0%

commit v1 on v0

v1 whole, which is shorter than its diff:
```python
import functools

import jax
import jax.numpy as jnp
from jax import lax
from jax.experimental import pallas as pl
from jax.experimental.pallas import tpu as pltpu
from jax.sharding import PartitionSpec as P

TN = (((0,), (0,)), ((), ()))


def tile_kernel(rows_ref, cols_ref, valid_ref, weight_ref, left_ref, right_ref, recorded_ref, out_ref):
    slot = pl.program_id(0)
    depth = left_ref.shape[0] * left_ref.shape[3]
    side = left_ref.shape[4]
    left_real = left_ref[:, 0, 0].reshape(depth, side).astype(jnp.float32)
    left_imag = left_ref[:, 0, 1].reshape(depth, side).astype(jnp.float32)
    w_real = weight_ref[0]
    w_imag = weight_ref[1]
    real_w = (w_real * left_real - w_imag * left_imag).astype(jnp.bfloat16)
    imag_w = (w_real * left_imag + w_imag * left_real).astype(jnp.bfloat16)
    right_real = right_ref[:, 0, 0].reshape(depth, side)
    right_imag = right_ref[:, 0, 1].reshape(depth, side)
    dot = functools.partial(lax.dot_general, dimension_numbers=TN, preferred_element_type=jnp.float32)
    real = dot(real_w, right_real) - dot(imag_w, right_imag)
    imag = dot(real_w, right_imag) + dot(imag_w, right_real)
    scale = valid_ref[slot].astype(jnp.float32)
    out_ref[0, 0] = recorded_ref[0, 0] - scale * real
    out_ref[0, 1] = recorded_ref[0, 1] - scale * imag


def tile_products(gathered, weight, rows, cols, valid, recorded):
    n_src, n_rcv, parts, depth, width = gathered.shape
    slots, _, side, _ = recorded.shape
    per_half = width // side
    half = (n_src, 1, parts, depth, side)
    flops = 8 * slots * side * side * n_src * depth
    return pl.pallas_call(
        tile_kernel,
        grid_spec=pltpu.PrefetchScalarGridSpec(
            num_scalar_prefetch=3,
            grid=(slots,),
            in_specs=[
                pl.BlockSpec((2, n_src * depth, side), lambda s, r, c, v: (0, 0, 0)),
                pl.BlockSpec(half, lambda s, r, c, v: (0, r[s] // per_half, 0, 0, r[s] % per_half)),
                pl.BlockSpec(half, lambda s, r, c, v: (0, c[s] // per_half, 0, 0, c[s] % per_half)),
                pl.BlockSpec((1, 2, side, side), lambda s, r, c, v: (s, 0, 0, 0)),
            ],
            out_specs=pl.BlockSpec((1, 2, side, side), lambda s, r, c, v: (s, 0, 0, 0)),
        ),
        out_shape=jax.ShapeDtypeStruct(recorded.shape, jnp.float32),
        compiler_params=pltpu.CompilerParams(vmem_limit_bytes=48 * 2**20),
        cost_estimate=pl.CostEstimate(flops=flops, bytes_accessed=50 * 2**20, transcendentals=0),
    )(rows, cols, valid, weight, gathered, gathered, recorded)


def body(panel, obliquity, panel_stations, tile_map, recorded):
    n_src = lax.axis_size("src")
    n_rcv = lax.axis_size("rcv")
    slots = recorded.shape[0]
    side = recorded.shape[2]
    gathered = lax.all_gather(panel.astype(jnp.bfloat16), ("src", "rcv"))
    gathered = gathered.reshape((n_src, n_rcv) + panel.shape)
    weight = jnp.take(obliquity, panel_stations, axis=1)
    weight = jnp.broadcast_to(weight[:, :, None], weight.shape + (side,))
    own = lax.axis_index("src") * n_rcv + lax.axis_index("rcv")
    mine = lax.dynamic_slice_in_dim(tile_map, own * slots, slots, 0)
    valid = (mine[:, 0] >= 0).astype(jnp.int32)
    rows = jnp.maximum(mine[:, 0], 0)
    cols = jnp.maximum(mine[:, 1], 0)
    return tile_products(gathered, weight, rows, cols, valid, recorded)


def solution(mesh):
    return jax.shard_map(
        body,
        mesh=mesh,
        in_specs=(
            P("freq", "src", "rcv"),
            P("freq", None),
            P(),
            P("freq", None),
            P(("src", "rcv"), "freq", None, None),
        ),
        out_specs=P(("src", "rcv"), "freq", None, None),
        check_vma=False,
    )
```

time: 886 us -> 166 us (0.19)
  waiting for transfers between devices: 561 us -> 79.9 us
  local copies, waits for them, and re-layouts: 192 us -> 41.7 us
  other arithmetic: 71.4 us -> 3.3 us
  matrix products: 33.7 us -> 0 us
  Pallas kernels: 0 us -> 25.7 us
  starting transfers between devices: 11.5 us -> 0.01 us
    all_to_all x2 -> x0, waiting for transfers between devices: 548 us -> none  [the longest x1 339 us: body(): lax.all_to_all(row_send, 'src', split_axis=2, concat_axis=1, tiled=True)]
    slice x9 -> x0, local copies, waits for them, and re-layouts: 121 us -> none  [the longest x3 57.2 us: tile_products(): left[0]]
    all_gather x1, waiting for transfers between devices: 12.7 us -> 79.9 us  [body(): gathered = lax.all_gather(panel.astype(jnp.bfloat16), ('src', 'rcv'))]
    dot_general x4 -> x0, matrix products: 33.7 us -> none  [the longest x1 9.03 us: tile_products(): jnp.einsum(form, weighted[1], right[1], preferred_element_type=jnp.float32)]
    select_n x5 -> x1, other arithmetic: 28.6 us -> 0.2 us  [body(): weight = jnp.take(obliquity, panel_stations, axis=1)]
    pallas_call x0 -> x1, Pallas kernels: none -> 25.7 us  [tile_products(): pl.pallas_call(tile_kernel, grid_spec=pltpu.PrefetchScalarGridSpec(num_sc...]
    gather x6 -> x1, local copies, waits for them, and re-layouts: 30.9 us -> 10.8 us  [body(): weight = jnp.take(obliquity, panel_stations, axis=1)]
    squeeze x1 -> x0, other arithmetic: 17.5 us -> none  [tile_products(): weighted[1]]
  transfers between devices with their start and end apart: 3 -> 1, of which waited for: 3 -> 1; matrix products, arithmetic and copies ran while one was open for 20% -> 25% of each run, Pallas kernels for 0% -> 0%
where the time goes in v1:
time: 166 us; the launch traced here: 164 us
  waiting for transfers between devices  79.9 us (48%)
  local copies, waits for them, and re-layouts  41.7 us (25%)
  Pallas kernels  25.7 us (15%)
  between operations  13.4 us (8%)
  other arithmetic  3.3 us (2%)
    all_gather x1, waiting for transfers between devices, body(): gathered = lax.all_gather(panel.astype(jnp.bfloat16), ('src', 'rcv'))  79.9 us
    unnamed x5, local copies, waits for them, and re-layouts  30.4 us
    pallas_call x1, Pallas kernels, tile_products(): pl.pallas_call(tile_kernel, grid_spec=pltpu.PrefetchScalarGridSpec(num_sc...  25.7 us
    gather x1, local copies, waits for them, and re-layouts, body(): weight = jnp.take(obliquity, panel_stations, axis=1)  10.8 us
  transfers between devices with their start and end apart: 1, of which 1 were waited for; matrix products, arithmetic and copies ran while one was open for 25% of the time, Pallas kernels for 0%

profile of v1, /device:TPU:0, one launch (start us, length us, event | category | flops | bytes accessed | tf_op | source)
XLA Modules:
  0.0 164.1 jit_solution(2211344541193859559)
XLA Ops:
  6.5 0.0 copy-start
  6.5 0.0 all-gather.3.cloned.1.call-start
  6.5 3.1 %convert_element_type.10 = bf16[2,128,2816]{2,1,0:T(8,128)(2,1)} convert(f32[2,128,2816]{2,1,0:T(8,128)} %param.5) | non-fusion elementwise | flops 720896 | bytes 4325376 | tf_op jit(solution)/shard_map/convert_element_type | solution.py:63
  9.6 0.0 all-gather.3.cloned.1.call-update
  9.6 0.0 copy-start.1
  9.7 30.3 %copy.8 = f32[2,131072]{0,1:T(8,128)} copy(f32[2,131072]{1,0:T(2,128)} %param.6) | data formatting | bytes 2097152 | tf_op args[1]
  40.0 0.0 copy-done.1
  40.0 10.8 %gather_fusion = f32[1024,2]{1,0:T(8,128)S(1)} fusion(f32[2,131072]{0,1:T(8,128)} %copy.8, s32[1024]{0:T(1024)S(1)} %fusion), kind=kCustom, calls=%fused_computation | custom fusion | bytes 20480 | tf_op jit(solution)/shard_map/jit(_take)/gather | solution.py:65
  50.8 0.2 select_bitcast_fusion
  51.0 0.2 copy.9
  51.2 0.0 copy-done
  51.2 0.1 constant_dynamic-slice_fusion
  51.3 79.9 %all-gather.3.cloned.1.call-done = bf16[32,128,2816]{2,1,0:T(8,128)(2,1)} async-done(((bf16[2,128,2816]{2,1,0:T(8,128)(2,1)}), bf16[32,128,2816]{2,1,0:T(8,128)(2,1)}) %all-gather.3.cloned.1.call-update) | async-done | bytes 23068688 | tf_op jit(solution)/shard_map/all_gather | solution.py:63
  131.2 0.3 broadcast_in_dim.21.weight_ref
  131.5 25.7 %shard_map.55 = f32[16,2,256,256]{3,2,1,0:T(8,128)} custom-call(s32[16]{0:T(128)S(1)} %get-tuple-element.6.rows_ref, s32[16]{0:T(128)S(1)} %get-tuple-element.5.cols_ref, s32[16]{0:T(128)S(1)} %fusion.1.valid_ref, f32[2,1024,256]{2,1,0:T(8,128)S(1)} %broadcast_in_dim.21.weight_ref, bf16[8,2,2,128,2816]{4,3,2,1,0:T(8,128)(2,1)} %bitcast.9, ...), custom_call_target="tpu_custom_call" | custom-call | flops 8589934592 | bytes 52428800 | tf_op jit(solution)/shard_map/pallas_call | solution.py:39
  (4 shorter events, 0.0 us)
Async XLA Ops:
  6.5 44.6 %copy-start = (s32[256,2]{0,1:T(2,128)S(1)}, s32[256,2]{0,1:T(2,128)}, u32[]{:S(2)}) copy-start(s32[256,2]{0,1:T(2,128)} %param.8) | copy-start | bytes 6148
  6.5 124.7 %all-gather.3.cloned.1.call-start = ((), (), s32[]{:S(2)}) async-start(), calls=%async_computation | async-start | bytes 24510464 | tf_op jit(solution)/shard_map/all_gather | solution.py:63
  9.6 30.4 %copy-start.1 = (s32[1024]{0:T(1024)S(1)}, s32[1024]{0:T(1024)}, u32[]{:S(2)}) copy-start(s32[1024]{0:T(1024)} %param.7) | copy-start | bytes 12292
Sparse Core Ops, SparseCore 0:
  9.8 121.4 all-gather.2

commit v2 on v0

v2 whole, which is shorter than its diff:
```python
import functools

import jax
import jax.numpy as jnp
from jax import lax
from jax.experimental import pallas as pl
from jax.experimental.pallas import tpu as pltpu
from jax.sharding import PartitionSpec as P

LANES = 128
COST = 1000
LIMIT = 16
GROUP = 2
ANY = pl.BlockSpec(memory_space=pl.ANY)
together = lax.optimization_barrier


def turn_kernel(_, kept_in, given_in, kept_out, given_out):
    for in_ref, out_ref in ((kept_in, kept_out), (given_in, given_out)):
        block = in_ref[...]
        out_ref[...] = block.reshape(block.shape[0] * block.shape[1], block.shape[2]).T.astype(jnp.bfloat16)


def turn(panel, rcv):
    parts, depth, width = panel.shape
    depth = depth // 2
    cols = width // 2
    out = jax.ShapeDtypeStruct((width, parts * depth), jnp.bfloat16)
    return pl.pallas_call(
        turn_kernel,
        grid_spec=pltpu.PrefetchScalarGridSpec(
            num_scalar_prefetch=1,
            grid=(width // cols,),
            in_specs=[
                pl.BlockSpec((parts, depth, cols), lambda c, r: (0, r[0], c)),
                pl.BlockSpec((parts, depth, cols), lambda c, r: (0, 1 - r[0], c)),
            ],
            out_specs=[pl.BlockSpec((cols, parts * depth), lambda c, r: (c, 0))] * 2,
        ),
        out_shape=[out, out],
        cost_estimate=pl.CostEstimate(flops=0, bytes_accessed=6 * panel.size, transcendentals=0),
    )(rcv[None], panel, panel)


def weights_kernel(stations_ref, line_ref, out_ref, table, sem):
    copies = [pltpu.make_async_copy(line_ref.at[:, part], table.at[part], sem.at[part]) for part in range(2)]
    for copy in copies:
        copy.start()
    stations = stations_ref[...]
    n_blocks = table.shape[1]
    block = lax.broadcasted_iota(jnp.int32, (n_blocks, stations.shape[1]), 0)
    pick = (block == stations // LANES).astype(jnp.float32).astype(jnp.bfloat16)
    lane = lax.broadcasted_iota(jnp.int32, (LANES, stations.shape[1]), 0)
    here = lane == stations % LANES
    for part in range(2):
        copies[part].wait()
        rest = table[part]
        total = None
        for _ in range(3):
            piece = rest.astype(jnp.bfloat16)
            rest = rest - piece.astype(jnp.float32)
            got = lax.dot_general(piece, pick, (((0,), (0,)), ((), ())), preferred_element_type=jnp.float32)
            total = got if total is None else total + got
        out_ref[pl.ds(part, 1), :] = jnp.sum(jnp.where(here, total, 0.0), axis=0, keepdims=True)


def station_weights(obliquity, stations):
    parts, line = obliquity.shape
    table = obliquity.reshape(parts, line // LANES, LANES).transpose(1, 0, 2)
    count = stations.shape[0]
    return pl.pallas_call(
        weights_kernel,
        in_specs=[pl.BlockSpec(memory_space=pltpu.VMEM), ANY],
        out_specs=pl.BlockSpec(memory_space=pltpu.VMEM),
        out_shape=jax.ShapeDtypeStruct((parts, count), jnp.float32),
        scratch_shapes=[pltpu.VMEM((parts, line // LANES, LANES), jnp.float32), pltpu.SemaphoreType.DMA((parts,))],
        compiler_params=pltpu.CompilerParams(vmem_limit_bytes=32 * 2**20),
        cost_estimate=pl.CostEstimate(flops=12 * line * count, bytes_accessed=4 * parts * line, transcendentals=0),
    )(stations[None, :], table)


def tiles_kernel(places, form, rows_ref, cols_ref, valid_ref, at_ref, *refs):
    n = len(places)
    pieces = refs[: 2 * n]
    weight_ref = refs[2 * n]
    refs = refs[2 * n + 1 :]
    acc_ref = got_ref = sem = None
    if form == "start":
        _, out_ref, token_ref = refs
    elif form == "last":
        acc_ref, got_ref, _, result_ref, out_ref, sem = refs
    else:
        acc_ref, _, out_ref, token_ref = refs
    if form != "last":
        token_ref[...] = jnp.zeros_like(token_ref)
    slots, _, side, _ = out_ref.shape
    per_half = pieces[0].shape[0] // side
    rcv = at_ref[0]
    shard = at_ref[1]
    half_lane = lax.broadcasted_iota(jnp.int32, (1, LANES), 1) < LANES // 2
    sign = jnp.where(half_lane, 1.0, -1.0)
    w_at = [lax.bitwise_xor(shard, relative) * 2 + lax.bitwise_xor(rcv, other) for relative, other in places]
    w_real = [weight_ref[0, pl.ds(index, 1), :] for index in w_at]
    w_imag = [weight_ref[1, pl.ds(index, 1), :] for index in w_at]

    def panel(piece, tile):
        place = pl.ds(pl.multiple_of(lax.rem(tile, per_half) * side, side), side)
        return jnp.where(tile // per_half == rcv, pieces[2 * piece][place, :], pieces[2 * piece + 1][place, :])

    def one_slot(slot):
        row = rows_ref[slot]
        col = cols_ref[slot]
        scale = valid_ref[slot].astype(jnp.float32)
        both = None
        for first in range(0, n, GROUP):
            upper, lower, right = [], [], []
            for p in range(first, min(first + GROUP, n)):
                value = panel(p, row).astype(jnp.float32)
                weighted = value * w_real[p] + pltpu.roll(value, LANES // 2, 1) * w_imag[p]
                upper.append((weighted * sign).astype(jnp.bfloat16))
                lower.append(pltpu.roll(weighted, LANES // 2, 1).astype(jnp.bfloat16))
                right.append(panel(p, col))
            left = jnp.concatenate([jnp.concatenate(upper, 1), jnp.concatenate(lower, 1)], 0)
            part = lax.dot_general(
                left, jnp.concatenate(right, 1), (((1,), (1,)), ((), ())), preferred_element_type=jnp.float32
            )
            both = part if both is None else both + part
        for part in range(2):
            value = -scale * both[part * side : (part + 1) * side]
            if acc_ref is not None:
                value = acc_ref[slot, part] + value
            if got_ref is not None:
                value = value + got_ref[slot, part].astype(jnp.float32)
            out_ref[slot, part] = value.astype(out_ref.dtype)
        if form == "last":
            pltpu.make_async_copy(out_ref.at[slot], result_ref.at[slot], sem.at[slot]).start()

    unroll = 4 if slots % 4 == 0 else 1

    @pl.loop(0, slots // unroll)
    def _(step):
        for i in range(unroll):
            one_slot(step * unroll + i)

    if form == "last":

        @pl.loop(0, slots)
        def _(slot):
            pltpu.make_async_copy(out_ref.at[slot], result_ref.at[slot], sem.at[slot]).wait()


def subtract(form, pieces, scalars, weights, shape, token, acc=None, got=None):
    n = len(pieces)
    places = [piece[:2] for piece in pieces]
    operands = [array for piece in pieces for array in piece[2:]] + [weights]
    operands += [array for array in (acc, got) if array is not None] + [token]
    vmem = pl.BlockSpec(memory_space=pltpu.VMEM)
    last = form == "last"
    result = jax.ShapeDtypeStruct(shape, jnp.float32)
    if form == "give":
        result = jax.ShapeDtypeStruct(shape, jnp.bfloat16)
    elif not last:
        result = pltpu.VMEM(shape, jnp.float32)
    return pl.pallas_call(
        functools.partial(tiles_kernel, places, form),
        in_specs=[pl.BlockSpec(memory_space=pltpu.SMEM)] * 4 + [vmem] * len(operands),
        out_specs=ANY if last else [vmem, vmem],
        scratch_shapes=[pltpu.VMEM(shape, jnp.float32), pltpu.SemaphoreType.DMA((shape[0],))] if last else [],
        out_shape=result if last else [result, jax.ShapeDtypeStruct((8, LANES), jnp.float32)],
        input_output_aliases={4 + 2 * n + 1: 0} if form == "add" else {},
        compiler_params=pltpu.CompilerParams(vmem_limit_bytes=LIMIT * 2**20),
        cost_estimate=pl.CostEstimate(flops=COST, bytes_accessed=COST, transcendentals=0),
    )(*scalars, *operands)


def body(panel, obliquity, panel_stations, tile_map, recorded):
    n_src = lax.axis_size("src")
    n_rcv = lax.axis_size("rcv")
    rcv = lax.axis_index("rcv")
    src = lax.axis_index("src")
    slots = recorded.shape[0]
    shards = 8
    span = n_src // shards
    if span > 1:
        groups = [[g * span + i for i in range(span)] for g in range(shards)]
        near = lax.all_gather(panel.astype(jnp.bfloat16), "src", axis=1, tiled=True, axis_index_groups=groups)
        panel = near.astype(jnp.float32)

    def send(a, distance):
        return lax.ppermute(a, "src", [(i, i ^ (distance * span)) for i in range(n_src)])

    def swap(a):
        return lax.ppermute(a, "rcv", [(0, 1), (1, 0)])

    def slots_of(device):
        mine = lax.dynamic_slice_in_dim(tile_map, device * slots, slots, 0)
        valid = (mine[:, 0] >= 0).astype(jnp.int32)
        place = jnp.stack([rcv, src // span]).astype(jnp.int32)
        return jnp.maximum(mine[:, 0], 0), jnp.maximum(mine[:, 1], 0), valid, place

    mine = slots_of(src * n_rcv + rcv)
    theirs = slots_of(src * n_rcv + 1 - rcv)
    w = station_weights(obliquity, panel_stations).reshape(2, shards * 2, -1)
    weights = jnp.stack([jnp.concatenate([w[0], w[0]], -1), jnp.concatenate([-w[1], w[1]], -1)])
    shape = recorded.shape
    token = jnp.zeros((8, LANES), jnp.float32)

    X, Z1, Z2 = 1, 2, 4
    h0, give = turn(panel, rcv)
    h1 = swap(give)
    A0 = send(h0, Z1)
    B0 = send(h0, Z2)
    X0 = send(h0, X)
    X1 = send(h1, X)
    A0, B0, X0, X1, h1, weights = together((A0, B0, X0, X1, h1, weights))

    A1 = send(h1, Z1)
    B1 = send(h1, Z2)
    XA0 = send(A0, X)
    XB0 = send(B0, X)
    pieces = [(0, 0, h0, h1), (X, 0, X0, X1)]
    away, token = subtract("start", pieces, theirs, weights, shape, token)
    home, token = subtract("first", pieces, mine, weights, shape, token, recorded)
    A1, B1, XA0, XB0, token = together((A1, B1, XA0, XB0, token))

    ZZ0 = send(B0, Z1)
    ZZ1 = send(B1, Z1)
    XB1 = send(B1, X)
    XA1 = send(A1, X)
    pieces = [(Z1, 0, A0, A1), (Z2, 0, B0, B1)]
    away, token = subtract("add", pieces, theirs, weights, shape, token, away)
    home, token = subtract("add", pieces, mine, weights, shape, token, home)
    ZZ0, ZZ1, XB1, XA1, token = together((ZZ0, ZZ1, XB1, XA1, token))

    XZZ0 = send(ZZ0, X)
    ZXB1 = send(XB1, Z1)
    pieces = [(Z1 + Z2, 0, ZZ0, ZZ1), (X + Z1, 0, XA0, XA1), (X + Z2, 0, XB0, XB1)]
    away, token = subtract("give", pieces, theirs, weights, shape, token, away)
    got = swap(away)
    home, token = subtract("add", pieces, mine, weights, shape, token, home)
    XZZ0, ZXB1, token = together((XZZ0, ZXB1, token))

    far = X + Z1 + Z2
    pieces = [(far, 0, XZZ0, ZXB1), (far, 1, swap(ZXB1), swap(XZZ0))]
    return subtract("last", pieces, mine, weights, shape, token, home, got)


def solution(mesh):
    return jax.shard_map(
        body,
        mesh=mesh,
        in_specs=(
            P("freq", "src", "rcv"),
            P("freq", None),
            P(),
            P("freq", None),
            P(("src", "rcv"), "freq", None, None),
        ),
        out_specs=P(("src", "rcv"), "freq", None, None),
        check_vma=False,
    )
```

time: 886 us -> 141 us (0.16)
  waiting for transfers between devices: 561 us -> 77.6 us
  local copies, waits for them, and re-layouts: 192 us -> 6.64 us
  other arithmetic: 71.4 us -> 0.17 us
  Pallas kernels: 0 us -> 36.9 us
  matrix products: 33.7 us -> 0 us
  between operations: 13.6 us -> 0.11 us
    all_to_all x2 -> x0, waiting for transfers between devices: 548 us -> none  [the longest x1 339 us: body(): lax.all_to_all(row_send, 'src', split_axis=2, concat_axis=1, tiled=True)]
    slice x9 -> x1, local copies, waits for them, and re-layouts: 121 us -> 0.03 us  [body(): w[0]]
    ppermute x0 -> x18, waiting for transfers between devices: none -> 77.6 us  [the longest x14 74.9 us: send(): lax.ppermute(a, 'src', [(i, i ^ distance * span) for i in range(n_src)])]
    pallas_call x0 -> x9, Pallas kernels: none -> 36.9 us  [the longest x7 30.6 us: subtract(): pl.pallas_call(functools.partial(tiles_kernel, places, form), in_specs=[p...]
    dot_general x4 -> x0, matrix products: 33.7 us -> none  [the longest x1 9.03 us: tile_products(): jnp.einsum(form, weighted[1], right[1], preferred_element_type=jnp.float32)]
    gather x6 -> x0, local copies, waits for them, and re-layouts: 30.9 us -> none  [the longest x1 10.5 us: body(): weight_k = jnp.take(obliquity, panel_stations, axis=1)]
    select_n x5 -> x0, other arithmetic: 28.6 us -> none  [the longest x2 14.2 us: body(): col_send = jnp.take(tiled, dest_cols, axis=2)]
    unnamed x16 -> x10, local copies, waits for them, and re-layouts: 32.9 us -> 6.4 us
  transfers between devices with their start and end apart: 3 -> 18, of which waited for: 3 -> 12; matrix products, arithmetic and copies ran while one was open for 20% -> 0% of each run, Pallas kernels for 0% -> 17%
where the time goes in v2:
time: 141 us; the launch traced here: 140 us
  waiting for transfers between devices  77.6 us (55%)
  Pallas kernels  36.9 us (26%)
  starting transfers between devices  19 us (13%)
  local copies, waits for them, and re-layouts  6.64 us (5%)
    ppermute x14, waiting for transfers between devices, send(): lax.ppermute(a, 'src', [(i, i ^ distance * span) for i in range(n_src)])  74.9 us
    pallas_call x7, Pallas kernels, subtract(): pl.pallas_call(functools.partial(tiles_kernel, places, form), in_specs=[p...  30.6 us
    ppermute x14, starting transfers between devices, send(): lax.ppermute(a, 'src', [(i, i ^ distance * span) for i in range(n_src)])  18 us
    unnamed x10, local copies, waits for them, and re-layouts  6.4 us
    pallas_call x1, Pallas kernels, station_weights(): pl.pallas_call(weights_kernel, in_specs=[pl.BlockSpec(memory_space=pltpu....  3.43 us
  transfers between devices with their start and end apart: 18, of which 12 were waited for; matrix products, arithmetic and copies ran while one was open for 0% of the time, Pallas kernels for 17%

profile of v2, /device:TPU:0, one launch (start us, length us, event | category | flops | bytes accessed | tf_op | source)
XLA Modules:
  0.0 140.4 jit_solution(501191271624322809)
XLA Ops:
  0.0 2.8 %shard_map.55 = (bf16[2816,128]{1,0:T(8,128)(2,1)}, bf16[2816,128]{1,0:T(8,128)(2,1)}) custom-call(s32[1]{0:T(128)} %bitcast.3._, f32[2,128,2816]{2,1,0:T(8,128)} %given_in.1, f32[2,128,2816]{2,1,0:T(8,128)} %given_in.1), custom_call_target="tpu_custom_call" | custom-call | bytes 4325376 | tf_op jit(solution)/shard_map/pallas_call | solution.py:29
  2.8 0.5 collective-permute-start.3
  3.3 2.6 %collective-permute-start = (bf16[2816,128]{1,0:T(8,128)(2,1)}, bf16[2816,128]{1,0:T(8,128)(2,1)S(1)}, u32[]{:S(2)}, u32[]{:S(2)}) collective-permute-start(bf16[2816,128]{1,0:T(8,128)(2,1)} %get-tuple-element.38.refs_0_), channel_id=1, source_target_pairs={{0,4},{2,6},{4,0},{6,2},{8,12},{10,14},{12,8},{14,10},{1,5},{3,7},... | collective-permute-start | bytes 2162696 | tf_op jit(solution)/shard_map/ppermute | solution.py:190
  5.9 2.6 %collective-permute-start.1 = (bf16[2816,128]{1,0:T(8,128)(2,1)}, bf16[2816,128]{1,0:T(8,128)(2,1)S(1)}, u32[]{:S(2)}, u32[]{:S(2)}) collective-permute-start(bf16[2816,128]{1,0:T(8,128)(2,1)} %get-tuple-element.38.refs_0_), channel_id=1, source_target_pairs={{0,8},{2,10},{4,12},{6,14},{8,0},{10,2},{12,4},{14,6},{1,9},{3,11}... | collective-permute-start | bytes 2162696 | tf_op jit(solution)/shard_map/ppermute | solution.py:190
  8.4 1.5 %collective-permute-start.2 = (bf16[2816,128]{1,0:T(8,128)(2,1)}, bf16[2816,128]{1,0:T(8,128)(2,1)S(1)}, u32[]{:S(2)}, u32[]{:S(2)}) collective-permute-start(bf16[2816,128]{1,0:T(8,128)(2,1)} %get-tuple-element.38.refs_0_), channel_id=1, source_target_pairs={{0,2},{2,0},{4,6},{6,4},{8,10},{10,8},{12,14},{14,12},{1,3},{3,1},... | collective-permute-start | bytes 2162696 | tf_op jit(solution)/shard_map/ppermute | solution.py:190
  9.9 0.5 collective-permute-start.4
  10.5 1.2 copy-done.2
  11.7 0.7 copy-done.3
  12.4 3.4 %shard_map.56 = f32[2,1024]{1,0:T(2,128)S(1)} custom-call(s32[1,1024]{1,0:T(1,128)S(1)} %bitcast.23, f32[1024,2,128]{2,1,0:T(2,128)S(1)} %bitcast.22), custom_call_target="tpu_custom_call" | custom-call | flops 1610612736 | bytes 1048576 | tf_op jit(solution)/shard_map/pallas_call | solution.py:71
  15.9 0.1 squeeze.5
  15.9 0.1 squeeze.4
  16.0 0.1 constant_dynamic-slice_fusion
  16.1 0.1 maximum_bitcast_fusion
  16.2 22.0 %collective-permute-done.refs_0_ = bf16[2816,128]{1,0:T(8,128)(2,1)S(1)} collective-permute-done((bf16[2816,128]{1,0:T(8,128)(2,1)}, bf16[2816,128]{1,0:T(8,128)(2,1)S(1)}, u32[]{:S(2)}, u32[]{:S(2)}) %collective-permute-start) | collective-permute-done | bytes 720928 | tf_op jit(solution)/shard_map/ppermute | solution.py:190
  38.2 2.6 %collective-permute-done.1.refs_2_ = bf16[2816,128]{1,0:T(8,128)(2,1)S(1)} collective-permute-done((bf16[2816,128]{1,0:T(8,128)(2,1)}, bf16[2816,128]{1,0:T(8,128)(2,1)S(1)}, u32[]{:S(2)}, u32[]{:S(2)}) %collective-permute-start.1) | collective-permute-done | bytes 720928 | tf_op jit(solution)/shard_map/ppermute | solution.py:190
  40.7 1.5 %collective-permute-done.4.refs_3_ = bf16[2816,128]{1,0:T(8,128)(2,1)} collective-permute-done((bf16[2816,128]{1,0:T(8,128)(2,1)S(1)}, bf16[2816,128]{1,0:T(8,128)(2,1)}, u32[]{:S(2)}, u32[]{:S(2)}) %collective-permute-start.4) | collective-permute-done | bytes 720928 | tf_op jit(solution)/shard_map/ppermute | solution.py:190
  42.2 0.4 collective-permute-start.6
  42.6 1.1 collective-permute-start.7
  43.8 1.5 %collective-permute-start.9 = (bf16[2816,128]{1,0:T(8,128)(2,1)S(1)}, bf16[2816,128]{1,0:T(8,128)(2,1)S(1)}, u32[]{:S(2)}, u32[]{:S(2)}) collective-permute-start(bf16[2816,128]{1,0:T(8,128)(2,1)S(1)} %collective-permute-done.1.refs_2_), channel_id=1, source_target_pairs={{0,2},{2,0},{4,6},{6,4},{8,10},{10,8},{12,14},{14,12},{1,3},{3,1},... | collective-permute-start | bytes 2162696 | tf_op jit(solution)/shard_map/ppermute | solution.py:190
  45.3 0.5 collective-permute-start.8
  45.8 0.1 pad_add_fusion.at_ref
  45.9 0.9 collective-permute-start.5
  46.7 1.1 copy-done.1
  47.9 3.7 %shard_map.57 = (f32[16,2,256,256]{3,2,1,0:T(8,128)S(1)}, f32[8,128]{1,0:T(8,128)S(1)}) custom-call(s32[16]{0:T(128)S(1)} %get-tuple-element.76.rows_ref, s32[16]{0:T(128)S(1)} %get-tuple-element.75.cols_ref, s32[16]{0:T(128)S(1)} %fusion.1.valid_ref, s32[2]{0:T(128)S(1)} %pad_add_fusion.at_ref, bf16[2816,128]{1,0:T(8,128)(2,1)S(1)} %copy-done.1, ...), custom_call_target="tpu_custom_call" | custom-call | flops 1000 | bytes 1000 | tf_op jit(solution)/shard_map/pallas_call | solution.py:164
  51.6 0.0 copy-start
  51.6 3.4 %copy-done = f32[16,2,256,256]{3,2,1,0:T(8,128)S(1)} copy-done((f32[16,2,256,256]{3,2,1,0:T(8,128)S(1)}, f32[16,2,256,256]{3,2,1,0:T(8,128)}, u32[]{:S(2)}) %copy-start) | copy-done | bytes 8388632
  55.0 3.8 %shard_map.58 = (f32[16,2,256,256]{3,2,1,0:T(8,128)S(1)}, f32[8,128]{1,0:T(8,128)S(1)}) custom-call(s32[16]{0:T(128)S(1)} %get-tuple-element.79.rows_ref, s32[16]{0:T(128)S(1)} %get-tuple-element.80.cols_ref, s32[16]{0:T(128)S(1)} %fusion.valid_ref, s32[2]{0:T(128)S(1)} %pad_add_fusion.at_ref, bf16[2816,128]{1,0:T(8,128)(2,1)S(1)} %copy-done.1, ...), custom_call_target="tpu_custom_call" | custom-call | flops 1000 | bytes 1000 | tf_op jit(solution)/shard_map/pallas_call | solution.py:164
  58.8 17.2 %collective-permute-done.6.refs_1_ = bf16[2816,128]{1,0:T(8,128)(2,1)S(1)} collective-permute-done((bf16[2816,128]{1,0:T(8,128)(2,1)S(1)}, bf16[2816,128]{1,0:T(8,128)(2,1)S(1)}, u32[]{:S(2)}, u32[]{:S(2)}) %collective-permute-start.6) | collective-permute-done | bytes 720928 | tf_op jit(solution)/shard_map/ppermute | solution.py:190
  76.0 0.1 collective-permute-done.8.refs_2_
  76.1 1.0 collective-permute-start.10
  77.1 1.5 %collective-permute-start.11 = (bf16[2816,128]{1,0:T(8,128)(2,1)S(1)}, bf16[2816,128]{1,0:T(8,128)(2,1)S(1)}, u32[]{:S(2)}, u32[]{:S(2)}) collective-permute-start(bf16[2816,128]{1,0:T(8,128)(2,1)S(1)} %collective-permute-done.7.refs_3_), channel_id=1, source_target_pairs={{0,2},{2,0},{4,6},{6,4},{8,10},{10,8},{12,14},{14,12},{1,3},{3,1},... | collective-permute-start | bytes 2162696 | tf_op jit(solution)/shard_map/ppermute | solution.py:190
  78.6 0.5 collective-permute-start.12
  79.1 4.0 %shard_map.59 = (f32[16,2,256,256]{3,2,1,0:T(8,128)S(1)}, f32[8,128]{1,0:T(8,128)S(1)}) custom-call(s32[16]{0:T(128)S(1)} %get-tuple-element.76.rows_ref, s32[16]{0:T(128)S(1)} %get-tuple-element.75.cols_ref, s32[16]{0:T(128)S(1)} %fusion.1.valid_ref, s32[2]{0:T(128)S(1)} %pad_add_fusion.at_ref, ...), custom_call_target="tpu_custom_call", output_to_operand_aliasing={{0}: (9, {})} | custom-call | flops 1000 | bytes 1000 | tf_op jit(solution)/shard_map/pallas_call | solution.py:164
  83.2 4.1 %shard_map.60 = (f32[16,2,256,256]{3,2,1,0:T(8,128)S(1)}, f32[8,128]{1,0:T(8,128)S(1)}) custom-call(s32[16]{0:T(128)S(1)} %get-tuple-element.79.rows_ref, s32[16]{0:T(128)S(1)} %get-tuple-element.80.cols_ref, s32[16]{0:T(128)S(1)} %fusion.valid_ref, s32[2]{0:T(128)S(1)} %pad_add_fusion.at_ref, ...), custom_call_target="tpu_custom_call", output_to_operand_aliasing={{0}: (9, {})} | custom-call | flops 1000 | bytes 1000 | tf_op jit(solution)/shard_map/pallas_call | solution.py:164
  87.3 4.2 %collective-permute-done.5.refs_0_ = bf16[2816,128]{1,0:T(8,128)(2,1)S(1)} collective-permute-done((bf16[2816,128]{1,0:T(8,128)(2,1)S(1)}, bf16[2816,128]{1,0:T(8,128)(2,1)S(1)}, u32[]{:S(2)}, u32[]{:S(2)}) %collective-permute-start.5) | collective-permute-done | bytes 720928 | tf_op jit(solution)/shard_map/ppermute | solution.py:190
  91.5 14.2 %collective-permute-done.10.refs_1_ = bf16[2816,128]{1,0:T(8,128)(2,1)S(1)} collective-permute-done((bf16[2816,128]{1,0:T(8,128)(2,1)S(1)}, bf16[2816,128]{1,0:T(8,128)(2,1)S(1)}, u32[]{:S(2)}, u32[]{:S(2)}) %collective-permute-start.10) | collective-permute-done | bytes 720928 | tf_op jit(solution)/shard_map/ppermute | solution.py:190
  105.7 1.9 %collective-permute-done.12.refs_3_ = bf16[2816,128]{1,0:T(8,128)(2,1)S(1)} collective-permute-done((bf16[2816,128]{1,0:T(8,128)(2,1)S(1)}, bf16[2816,128]{1,0:T(8,128)(2,1)S(1)}, u32[]{:S(2)}, u32[]{:S(2)}) %collective-permute-start.12) | collective-permute-done | bytes 720928 | tf_op jit(solution)/shard_map/ppermute | solution.py:190
  107.5 4.6 %shard_map.61 = (bf16[16,2,256,256]{3,2,1,0:T(8,128)(2,1)S(1)}, f32[8,128]{1,0:T(8,128)S(1)}) custom-call(s32[16]{0:T(128)S(1)} %get-tuple-element.76.rows_ref, s32[16]{0:T(128)S(1)} %get-tuple-element.75.cols_ref, s32[16]{0:T(128)S(1)} %fusion.1.valid_ref, s32[2]{0:T(128)S(1)} %pad_add_fusion.at_ref, bf16[2816,128]{1,0:T(8,128)(2,1)S(1)} %collective-permute-done.5.refs_0_, ...), custom_call_target="tpu_custom_call" | custom-call | flops 1000 | bytes 1000 | tf_op jit(solution)/shard_map/pallas_call | solution.py:164
  112.2 0.1 collective-permute-start.17
  112.2 1.6 %collective-permute-start.13 = (bf16[2816,128]{1,0:T(8,128)(2,1)S(1)}, bf16[2816,128]{1,0:T(8,128)(2,1)S(1)}, u32[]{:S(2)}, u32[]{:S(2)}) collective-permute-start(bf16[2816,128]{1,0:T(8,128)(2,1)S(1)} %collective-permute-done.5.refs_0_), channel_id=1, source_target_pairs={{0,2},{2,0},{4,6},{6,4},{8,10},{10,8},{12,14},{14,12},{1,3},{3,1},... | collective-permute-start | bytes 2162696 | tf_op jit(solution)/shard_map/ppermute | solution.py:190
  113.8 1.7 %collective-permute-start.14 = (bf16[2816,128]{1,0:T(8,128)(2,1)S(1)}, bf16[2816,128]{1,0:T(8,128)(2,1)S(1)}, u32[]{:S(2)}, u32[]{:S(2)}) collective-permute-start(bf16[2816,128]{1,0:T(8,128)(2,1)S(1)} %collective-permute-done.11.refs_5_), channel_id=1, source_target_pairs={{0,4},{2,6},{4,0},{6,2},{8,12},{10,14},{12,8},{14,10},{1,5},{3,7},... | collective-permute-start | bytes 2162696 | tf_op jit(solution)/shard_map/ppermute | solution.py:190
  115.5 5.2 %shard_map.62 = (f32[16,2,256,256]{3,2,1,0:T(8,128)S(1)}, f32[8,128]{1,0:T(8,128)S(1)}) custom-call(s32[16]{0:T(128)S(1)} %get-tuple-element.79.rows_ref, s32[16]{0:T(128)S(1)} %get-tuple-element.80.cols_ref, s32[16]{0:T(128)S(1)} %fusion.valid_ref, s32[2]{0:T(128)S(1)} %pad_add_fusion.at_ref, ...), custom_call_target="tpu_custom_call", output_to_operand_aliasing={{0}: (11, {})} | custom-call | flops 1000 | bytes 1000 | tf_op jit(solution)/shard_map/pallas_call | solution.py:164
  120.7 10.0 %collective-permute-done.13.refs_0_ = bf16[2816,128]{1,0:T(8,128)(2,1)S(1)} collective-permute-done((bf16[2816,128]{1,0:T(8,128)(2,1)S(1)}, bf16[2816,128]{1,0:T(8,128)(2,1)S(1)}, u32[]{:S(2)}, u32[]{:S(2)}) %collective-permute-start.13) | collective-permute-done | bytes 720928 | tf_op jit(solution)/shard_map/ppermute | solution.py:190
  130.8 1.2 collective-permute-done.14.refs_1_
  132.0 0.5 collective-permute-start.16
  132.5 1.7 %collective-permute-done.15.refs_2_ = bf16[2816,128]{1,0:T(8,128)(2,1)S(1)} collective-permute-done((bf16[2816,128]{1,0:T(8,128)(2,1)S(1)}, bf16[2816,128]{1,0:T(8,128)(2,1)S(1)}, u32[]{:S(2)}, u32[]{:S(2)}) %collective-permute-start.15) | collective-permute-done | bytes 720928 | tf_op jit(solution)/shard_map/ppermute | solution.py:193
  134.2 1.0 collective-permute-done.16.refs_3_
  135.2 5.2 %shard_map.63 = f32[16,2,256,256]{3,2,1,0:T(8,128)} custom-call(s32[16]{0:T(128)S(1)} %get-tuple-element.79.rows_ref, s32[16]{0:T(128)S(1)} %get-tuple-element.80.cols_ref, s32[16]{0:T(128)S(1)} %fusion.valid_ref, s32[2]{0:T(128)S(1)} %pad_add_fusion.at_ref, bf16[2816,128]{1,0:T(8,128)(2,1)S(1)} %collective-permute-done.13.refs_0_, ...), custom_call_target="tpu_custom_call" | custom-call | flops 1000 | bytes 1000 | tf_op jit(solution)/shard_map/pallas_call | solution.py:164
  (19 shorter events, 0.1 us)
Async XLA Ops:
  0.0 16.0 %copy-start.4 = (s32[256,2]{0,1:T(2,128)S(1)}, s32[256,2]{0,1:T(2,128)}, u32[]{:S(2)}) copy-start(s32[256,2]{0,1:T(2,128)} %param.8) | copy-start | bytes 6148
  2.8 7.1 %collective-permute-start.3 = (bf16[2816,128]{1,0:T(8,128)(2,1)}, bf16[2816,128]{1,0:T(8,128)(2,1)S(1)}, u32[]{:S(2)}, u32[]{:S(2)}) collective-permute-start(bf16[2816,128]{1,0:T(8,128)(2,1)} %get-tuple-element.39), channel_id=1, source_target_pairs={{0,1},{1,0},{2,3},{3,2},{4,5},{5,4},{6,7},{7,6},{8,9},{9,8},{10,11... | collective-permute-start | bytes 2162696 | tf_op jit(solution)/shard_map/ppermute | solution.py:193
  3.3 34.9 %collective-permute-start = (bf16[2816,128]{1,0:T(8,128)(2,1)}, bf16[2816,128]{1,0:T(8,128)(2,1)S(1)}, u32[]{:S(2)}, u32[]{:S(2)}) collective-permute-start(bf16[2816,128]{1,0:T(8,128)(2,1)} %get-tuple-element.38.refs_0_), channel_id=1, source_target_pairs={{0,4},{2,6},{4,0},{6,2},{8,12},{10,14},{12,8},{14,10},{1,5},{3,7},... | collective-permute-start | bytes 2162696 | tf_op jit(solution)/shard_map/ppermute | solution.py:190
  5.9 34.9 %collective-permute-start.1 = (bf16[2816,128]{1,0:T(8,128)(2,1)}, bf16[2816,128]{1,0:T(8,128)(2,1)S(1)}, u32[]{:S(2)}, u32[]{:S(2)}) collective-permute-start(bf16[2816,128]{1,0:T(8,128)(2,1)} %get-tuple-element.38.refs_0_), channel_id=1, source_target_pairs={{0,8},{2,10},{4,12},{6,14},{8,0},{10,2},{12,4},{14,6},{1,9},{3,11}... | collective-permute-start | bytes 2162696 | tf_op jit(solution)/shard_map/ppermute | solution.py:190
  8.4 32.3 %collective-permute-start.2 = (bf16[2816,128]{1,0:T(8,128)(2,1)}, bf16[2816,128]{1,0:T(8,128)(2,1)S(1)}, u32[]{:S(2)}, u32[]{:S(2)}) collective-permute-start(bf16[2816,128]{1,0:T(8,128)(2,1)} %get-tuple-element.38.refs_0_), channel_id=1, source_target_pairs={{0,2},{2,0},{4,6},{6,4},{8,10},{10,8},{12,14},{14,12},{1,3},{3,1},... | collective-permute-start | bytes 2162696 | tf_op jit(solution)/shard_map/ppermute | solution.py:190
  9.9 32.3 %collective-permute-start.4 = (bf16[2816,128]{1,0:T(8,128)(2,1)S(1)}, bf16[2816,128]{1,0:T(8,128)(2,1)}, u32[]{:S(2)}, u32[]{:S(2)}) collective-permute-start(bf16[2816,128]{1,0:T(8,128)(2,1)S(1)} %collective-permute-done.3.refs_1_), channel_id=1, source_target_pairs={{0,2},{2,0},{4,6},{6,4},{8,10},{10,8},{12,14},{14,12},{1,3},{3,1},... | collective-permute-start | bytes 2162696 | tf_op jit(solution)/shard_map/ppermute | solution.py:190
  10.5 1.2 copy-start.2
  11.7 0.7 copy-start.3
  42.2 33.8 %collective-permute-start.6 = (bf16[2816,128]{1,0:T(8,128)(2,1)S(1)}, bf16[2816,128]{1,0:T(8,128)(2,1)S(1)}, u32[]{:S(2)}, u32[]{:S(2)}) collective-permute-start(bf16[2816,128]{1,0:T(8,128)(2,1)S(1)} %collective-permute-done.3.refs_1_), channel_id=1, source_target_pairs={{0,4},{2,6},{4,0},{6,2},{8,12},{10,14},{12,8},{14,10},{1,5},{3,7},... | collective-permute-start | bytes 2162696 | tf_op jit(solution)/shard_map/ppermute | solution.py:190
  42.6 33.4 %collective-permute-start.7 = (bf16[2816,128]{1,0:T(8,128)(2,1)S(1)}, bf16[2816,128]{1,0:T(8,128)(2,1)S(1)}, u32[]{:S(2)}, u32[]{:S(2)}) collective-permute-start(bf16[2816,128]{1,0:T(8,128)(2,1)S(1)} %collective-permute-done.3.refs_1_), channel_id=1, source_target_pairs={{0,8},{2,10},{4,12},{6,14},{8,0},{10,2},{12,4},{14,6},{1,9},{3,11}... | collective-permute-start | bytes 2162696 | tf_op jit(solution)/shard_map/ppermute | solution.py:190
  43.8 32.2 %collective-permute-start.9 = (bf16[2816,128]{1,0:T(8,128)(2,1)S(1)}, bf16[2816,128]{1,0:T(8,128)(2,1)S(1)}, u32[]{:S(2)}, u32[]{:S(2)}) collective-permute-start(bf16[2816,128]{1,0:T(8,128)(2,1)S(1)} %collective-permute-done.1.refs_2_), channel_id=1, source_target_pairs={{0,2},{2,0},{4,6},{6,4},{8,10},{10,8},{12,14},{14,12},{1,3},{3,1},... | collective-permute-start | bytes 2162696 | tf_op jit(solution)/shard_map/ppermute | solution.py:190
  45.3 30.8 %collective-permute-start.8 = (bf16[2816,128]{1,0:T(8,128)(2,1)S(1)}, bf16[2816,128]{1,0:T(8,128)(2,1)S(1)}, u32[]{:S(2)}, u32[]{:S(2)}) collective-permute-start(bf16[2816,128]{1,0:T(8,128)(2,1)S(1)} %collective-permute-done.refs_0_), channel_id=1, source_target_pairs={{0,2},{2,0},{4,6},{6,4},{8,10},{10,8},{12,14},{14,12},{1,3},{3,1},... | collective-permute-start | bytes 2162696 | tf_op jit(solution)/shard_map/ppermute | solution.py:190
  45.9 45.6 %collective-permute-start.5 = (bf16[2816,128]{1,0:T(8,128)(2,1)S(1)}, bf16[2816,128]{1,0:T(8,128)(2,1)S(1)}, u32[]{:S(2)}, u32[]{:S(2)}) collective-permute-start(bf16[2816,128]{1,0:T(8,128)(2,1)S(1)} %collective-permute-done.1.refs_2_), channel_id=1, source_target_pairs={{0,4},{2,6},{4,0},{6,2},{8,12},{10,14},{12,8},{14,10},{1,5},{3,7},... | collective-permute-start | bytes 2162696 | tf_op jit(solution)/shard_map/ppermute | solution.py:190
  46.7 1.1 copy-start.1
  51.6 3.4 %copy-start = (f32[16,2,256,256]{3,2,1,0:T(8,128)S(1)}, f32[16,2,256,256]{3,2,1,0:T(8,128)}, u32[]{:S(2)}) copy-start(f32[16,2,256,256]{3,2,1,0:T(8,128)} %refs_5_.1) | copy-start | bytes 25165828
  76.1 29.6 %collective-permute-start.10 = (bf16[2816,128]{1,0:T(8,128)(2,1)S(1)}, bf16[2816,128]{1,0:T(8,128)(2,1)S(1)}, u32[]{:S(2)}, u32[]{:S(2)}) collective-permute-start(bf16[2816,128]{1,0:T(8,128)(2,1)S(1)} %collective-permute-done.7.refs_3_), channel_id=1, source_target_pairs={{0,4},{2,6},{4,0},{6,2},{8,12},{10,14},{12,8},{14,10},{1,5},{3,7},... | collective-permute-start | bytes 2162696 | tf_op jit(solution)/shard_map/ppermute | solution.py:190
  77.1 28.6 %collective-permute-start.11 = (bf16[2816,128]{1,0:T(8,128)(2,1)S(1)}, bf16[2816,128]{1,0:T(8,128)(2,1)S(1)}, u32[]{:S(2)}, u32[]{:S(2)}) collective-permute-start(bf16[2816,128]{1,0:T(8,128)(2,1)S(1)} %collective-permute-done.7.refs_3_), channel_id=1, source_target_pairs={{0,2},{2,0},{4,6},{6,4},{8,10},{10,8},{12,14},{14,12},{1,3},{3,1},... | collective-permute-start | bytes 2162696 | tf_op jit(solution)/shard_map/ppermute | solution.py:190
  78.6 28.9 %collective-permute-start.12 = (bf16[2816,128]{1,0:T(8,128)(2,1)S(1)}, bf16[2816,128]{1,0:T(8,128)(2,1)S(1)}, u32[]{:S(2)}, u32[]{:S(2)}) collective-permute-start(bf16[2816,128]{1,0:T(8,128)(2,1)S(1)} %collective-permute-done.6.refs_1_), channel_id=1, source_target_pairs={{0,2},{2,0},{4,6},{6,4},{8,10},{10,8},{12,14},{14,12},{1,3},{3,1},... | collective-permute-start | bytes 2162696 | tf_op jit(solution)/shard_map/ppermute | solution.py:190
  112.2 23.1 %collective-permute-start.17 = (bf16[16,2,256,256]{3,2,1,0:T(8,128)(2,1)S(1)}, bf16[16,2,256,256]{3,2,1,0:T(8,128)(2,1)S(1)}, u32[]{:S(2)}, u32[]{:S(2)}) collective-permute-start(bf16[16,2,256,256]{3,2,1,0:T(8,128)(2,1)S(1)} %get-tuple-element.69), channel_id=1, source_target_pairs={{0,1},{1,0},{2,3},{3,2},{4,5},{5,4},{6,7},{7,6},{8,9},{9,8},{10,11... | collective-permute-start | bytes 12582920 | tf_op jit(solution)/shard_map/ppermute | solution.py:193
  112.2 18.6 %collective-permute-start.13 = (bf16[2816,128]{1,0:T(8,128)(2,1)S(1)}, bf16[2816,128]{1,0:T(8,128)(2,1)S(1)}, u32[]{:S(2)}, u32[]{:S(2)}) collective-permute-start(bf16[2816,128]{1,0:T(8,128)(2,1)S(1)} %collective-permute-done.5.refs_0_), channel_id=1, source_target_pairs={{0,2},{2,0},{4,6},{6,4},{8,10},{10,8},{12,14},{14,12},{1,3},{3,1},... | collective-permute-start | bytes 2162696 | tf_op jit(solution)/shard_map/ppermute | solution.py:190
  113.8 18.2 %collective-permute-start.14 = (bf16[2816,128]{1,0:T(8,128)(2,1)S(1)}, bf16[2816,128]{1,0:T(8,128)(2,1)S(1)}, u32[]{:S(2)}, u32[]{:S(2)}) collective-permute-start(bf16[2816,128]{1,0:T(8,128)(2,1)S(1)} %collective-permute-done.11.refs_5_), channel_id=1, source_target_pairs={{0,4},{2,6},{4,0},{6,2},{8,12},{10,14},{12,8},{14,10},{1,5},{3,7},... | collective-permute-start | bytes 2162696 | tf_op jit(solution)/shard_map/ppermute | solution.py:190
  132.0 2.2 %collective-permute-start.15 = (bf16[2816,128]{1,0:T(8,128)(2,1)S(1)}, bf16[2816,128]{1,0:T(8,128)(2,1)S(1)}, u32[]{:S(2)}, u32[]{:S(2)}) collective-permute-start(bf16[2816,128]{1,0:T(8,128)(2,1)S(1)} %collective-permute-done.14.refs_1_), channel_id=1, source_target_pairs={{0,1},{1,0},{2,3},{3,2},{4,5},{5,4},{6,7},{7,6},{8,9},{9,8},{10,11... | collective-permute-start | bytes 2162696 | tf_op jit(solution)/shard_map/ppermute | solution.py:193
  132.0 3.2 %collective-permute-start.16 = (bf16[2816,128]{1,0:T(8,128)(2,1)S(1)}, bf16[2816,128]{1,0:T(8,128)(2,1)S(1)}, u32[]{:S(2)}, u32[]{:S(2)}) collective-permute-start(bf16[2816,128]{1,0:T(8,128)(2,1)S(1)} %collective-permute-done.13.refs_0_), channel_id=1, source_target_pairs={{0,1},{1,0},{2,3},{3,2},{4,5},{5,4},{6,7},{7,6},{8,9},{9,8},{10,11... | collective-permute-start | bytes 2162696 | tf_op jit(solution)/shard_map/ppermute | solution.py:193

commit v3 on v2

--- a/solution.py
+++ b/solution.py
@@ -79,26 +79,29 @@
     )(stations[None, :], table)
 
 
-def tiles_kernel(places, form, rows_ref, cols_ref, valid_ref, at_ref, *refs):
+def tiles_kernel(places, form, unroll, rows_ref, cols_ref, valid_ref, at_ref, *refs):
     n = len(places)
     pieces = refs[: 2 * n]
     weight_ref = refs[2 * n]
     refs = refs[2 * n + 1 :]
-    acc_ref = got_ref = sem = None
+    acc_ref = None
+    got_refs = ()
     if form == "start":
         _, out_ref, token_ref = refs
     elif form == "last":
-        acc_ref, got_ref, _, result_ref, out_ref, sem = refs
+        acc_ref, *got_refs, _, result_ref, out_ref, sem = refs
     else:
-        acc_ref, _, out_ref, token_ref = refs
+        acc_ref, _, *outs, token_ref = refs
+        out_ref = outs[0]
     if form != "last":
         token_ref[...] = jnp.zeros_like(token_ref)
-    slots, _, side, _ = out_ref.shape
+    slots = rows_ref.shape[0]
+    side = out_ref.shape[2]
     per_half = pieces[0].shape[0] // side
     rcv = at_ref[0]
     shard = at_ref[1]
     half_lane = lax.broadcasted_iota(jnp.int32, (1, LANES), 1) < LANES // 2
-    sign = jnp.where(half_lane, 1.0, -1.0)
+    sign = jnp.where(half_lane, 1.0, -1.0).astype(jnp.bfloat16)
     w_at = [lax.bitwise_xor(shard, relative) * 2 + lax.bitwise_xor(rcv, other) for relative, other in places]
     w_real = [weight_ref[0, pl.ds(index, 1), :] for index in w_at]
     w_imag = [weight_ref[1, pl.ds(index, 1), :] for index in w_at]
@@ -107,18 +110,19 @@
         place = pl.ds(pl.multiple_of(lax.rem(tile, per_half) * side, side), side)
         return jnp.where(tile // per_half == rcv, pieces[2 * piece][place, :], pieces[2 * piece + 1][place, :])
 
-    def one_slot(slot):
+    def one_slot(slot, step, i):
         row = rows_ref[slot]
         col = cols_ref[slot]
-        scale = valid_ref[slot].astype(jnp.float32)
+        scale = -valid_ref[slot].astype(jnp.float32)
         both = None
         for first in range(0, n, GROUP):
             upper, lower, right = [], [], []
             for p in range(first, min(first + GROUP, n)):
                 value = panel(p, row).astype(jnp.float32)
-                weighted = value * w_real[p] + pltpu.roll(value, LANES // 2, 1) * w_imag[p]
-                upper.append((weighted * sign).astype(jnp.bfloat16))
-                lower.append(pltpu.roll(weighted, LANES // 2, 1).astype(jnp.bfloat16))
+                weighted = value * (scale * w_real[p]) + pltpu.roll(value, LANES // 2, 1) * (scale * w_imag[p])
+                weighted = weighted.astype(jnp.bfloat16)
+                upper.append(weighted * sign)
+                lower.append(pltpu.roll(weighted, LANES // 2, 1))
                 right.append(panel(p, col))
             left = jnp.concatenate([jnp.concatenate(upper, 1), jnp.concatenate(lower, 1)], 0)
             part = lax.dot_general(
@@ -126,21 +130,27 @@
             )
             both = part if both is None else both + part
         for part in range(2):
-            value = -scale * both[part * side : (part + 1) * side]
+            value = both[part * side : (part + 1) * side]
             if acc_ref is not None:
                 value = acc_ref[slot, part] + value
-            if got_ref is not None:
-                value = value + got_ref[slot, part].astype(jnp.float32)
-            out_ref[slot, part] = value.astype(out_ref.dtype)
+            if got_refs:
+                value = value + got_refs[i][step, part].astype(jnp.float32)
+            if form == "give":
+                outs[i][step, part] = value.astype(out_ref.dtype)
+            else:
+                out_ref[slot, part] = value
         if form == "last":
             pltpu.make_async_copy(out_ref.at[slot], result_ref.at[slot], sem.at[slot]).start()
 
-    unroll = 4 if slots % 4 == 0 else 1
-
-    @pl.loop(0, slots // unroll)
-    def _(step):
-        for i in range(unroll):
-            one_slot(step * unroll + i)
+    steps = slots // unroll
+
+    group = unroll // 2 if form == "last" and unroll > 1 else unroll
+    for base in range(0, unroll, group):
+
+        @pl.loop(0, steps)
+        def _(step):
+            for i in range(base, base + group):
+                one_slot(i * steps + step, step, i)
 
     if form == "last":
 
@@ -149,24 +159,25 @@
             pltpu.make_async_copy(out_ref.at[slot], result_ref.at[slot], sem.at[slot]).wait()
 
 
-def subtract(form, pieces, scalars, weights, shape, token, acc=None, got=None):
+def subtract(form, pieces, scalars, weights, shape, token, acc=None, got=()):
     n = len(pieces)
     places = [piece[:2] for piece in pieces]
     operands = [array for piece in pieces for array in piece[2:]] + [weights]
-    operands += [array for array in (acc, got) if array is not None] + [token]
+    operands += ([] if acc is None else [acc]) + list(got) + [token]
     vmem = pl.BlockSpec(memory_space=pltpu.VMEM)
     last = form == "last"
+    unroll = 8 if shape[0] % 8 == 0 else 1
     result = jax.ShapeDtypeStruct(shape, jnp.float32)
     if form == "give":
-        result = jax.ShapeDtypeStruct(shape, jnp.bfloat16)
+        result = [jax.ShapeDtypeStruct((shape[0] // unroll,) + shape[1:], jnp.bfloat16)] * unroll
     elif not last:
         result = pltpu.VMEM(shape, jnp.float32)
     return pl.pallas_call(
-        functools.partial(tiles_kernel, places, form),
+        functools.partial(tiles_kernel, places, form, unroll),
         in_specs=[pl.BlockSpec(memory_space=pltpu.SMEM)] * 4 + [vmem] * len(operands),
-        out_specs=ANY if last else [vmem, vmem],
+        out_specs=ANY if last else [vmem] * (1 + (unroll if form == "give" else 1)),
         scratch_shapes=[pltpu.VMEM(shape, jnp.float32), pltpu.SemaphoreType.DMA((shape[0],))] if last else [],
-        out_shape=result if last else [result, jax.ShapeDtypeStruct((8, LANES), jnp.float32)],
+        out_shape=result if last else [*(result if form == "give" else [result]), jax.ShapeDtypeStruct((8, LANES), jnp.float32)],
         input_output_aliases={4 + 2 * n + 1: 0} if form == "add" else {},
         compiler_params=pltpu.CompilerParams(vmem_limit_bytes=LIMIT * 2**20),
         cost_estimate=pl.CostEstimate(flops=COST, bytes_accessed=COST, transcendentals=0),
@@ -212,7 +223,7 @@
     B0 = send(h0, Z2)
     X0 = send(h0, X)
     X1 = send(h1, X)
-    A0, B0, X0, X1, h1, weights = together((A0, B0, X0, X1, h1, weights))
+    A0, B0, X0, X1, weights = together((A0, B0, X0, X1, weights))
 
     A1 = send(h1, Z1)
     B1 = send(h1, Z2)
@@ -227,17 +238,17 @@
     ZZ1 = send(B1, Z1)
     XB1 = send(B1, X)
     XA1 = send(A1, X)
-    pieces = [(Z1, 0, A0, A1), (Z2, 0, B0, B1)]
+    pieces = [(Z1, 0, A0, A1), (Z2, 0, B0, B1), (X + Z2, 0, XB0, XB1)]
     away, token = subtract("add", pieces, theirs, weights, shape, token, away)
     home, token = subtract("add", pieces, mine, weights, shape, token, home)
-    ZZ0, ZZ1, XB1, XA1, token = together((ZZ0, ZZ1, XB1, XA1, token))
+    ZZ1, XA1, token = together((ZZ1, XA1, token))
 
     XZZ0 = send(ZZ0, X)
     ZXB1 = send(XB1, Z1)
-    pieces = [(Z1 + Z2, 0, ZZ0, ZZ1), (X + Z1, 0, XA0, XA1), (X + Z2, 0, XB0, XB1)]
-    away, token = subtract("give", pieces, theirs, weights, shape, token, away)
-    got = swap(away)
+    pieces = [(Z1 + Z2, 0, ZZ0, ZZ1), (X + Z1, 0, XA0, XA1)]
     home, token = subtract("add", pieces, mine, weights, shape, token, home)
+    *away, token = subtract("give", pieces, theirs, weights, shape, token, away)
+    got = [swap(a) for a in away]
     XZZ0, ZXB1, token = together((XZZ0, ZXB1, token))
 
     far = X + Z1 + Z2

time: 141 us -> 134 us (0.950)
  waiting for transfers between devices: 77.6 us -> 73.2 us
  Pallas kernels: 36.9 us -> 35.1 us
    ppermute x14, waiting for transfers between devices: 74.9 us -> 67.6 us  [send(): lax.ppermute(a, 'src', [(i, i ^ distance * span) for i in range(n_src)])]
    ppermute x4 -> x11, waiting for transfers between devices: 2.72 us -> 5.6 us  [swap(): return lax.ppermute(a, 'rcv', [(0, 1), (1, 0)])]
    ppermute x14, starting transfers between devices: 18 us -> 16.1 us  [send(): lax.ppermute(a, 'src', [(i, i ^ distance * span) for i in range(n_src)])]
    pallas_call x7, Pallas kernels: 30.6 us -> 28.9 us  [subtract(): pl.pallas_call(functools.partial(tiles_kernel, places, form, unroll), in_...]
    ppermute x4 -> x11, starting transfers between devices: 1.05 us -> 2.49 us  [swap(): return lax.ppermute(a, 'rcv', [(0, 1), (1, 0)])]
  transfers between devices with their start and end apart: 18 -> 25, of which waited for: 12 -> 15; matrix products, arithmetic and copies ran while one was open for 0% -> 0% of each run, Pallas kernels for 17% -> 20%
where the time goes in v3:
time: 134 us
  waiting for transfers between devices  73.2 us (55%)
  Pallas kernels  35.1 us (26%)
  starting transfers between devices  18.6 us (14%)
  local copies, waits for them, and re-layouts  6.64 us (5%)
    ppermute x14, waiting for transfers between devices, send(): lax.ppermute(a, 'src', [(i, i ^ distance * span) for i in range(n_src)])  67.6 us
    pallas_call x7, Pallas kernels, subtract(): pl.pallas_call(functools.partial(tiles_kernel, places, form, unroll), in_...  28.9 us
    ppermute x14, starting transfers between devices, send(): lax.ppermute(a, 'src', [(i, i ^ distance * span) for i in range(n_src)])  16.1 us
    unnamed x10, local copies, waits for them, and re-layouts  6.4 us
    ppermute x11, waiting for transfers between devices, swap(): return lax.ppermute(a, 'rcv', [(0, 1), (1, 0)])  5.6 us
    pallas_call x1, Pallas kernels, station_weights(): pl.pallas_call(weights_kernel, in_specs=[pl.BlockSpec(memory_space=pltpu....  3.43 us
    pallas_call x1, Pallas kernels, turn(): pl.pallas_call(turn_kernel, grid_spec=pltpu.PrefetchScalarGridSpec(num_sc...  2.82 us
  transfers between devices with their start and end apart: 25, of which 15 were waited for; matrix products, arithmetic and copies ran while one was open for 0% of the time, Pallas kernels for 20%

profile of v3, /device:TPU:0, one launch (start us, length us, event | category | flops | bytes accessed | tf_op | source)
XLA Modules:
  0.0 134.0 jit_solution(1826740678340553907)
XLA Ops:
  0.0 2.8 %shard_map.55 = (bf16[2816,128]{1,0:T(8,128)(2,1)}, bf16[2816,128]{1,0:T(8,128)(2,1)}) custom-call(s32[1]{0:T(128)} %bitcast.3._, f32[2,128,2816]{2,1,0:T(8,128)} %given_in.1, f32[2,128,2816]{2,1,0:T(8,128)} %given_in.1), custom_call_target="tpu_custom_call" | custom-call | bytes 4325376 | tf_op jit(solution)/shard_map/pallas_call | solution.py:29
  2.8 0.5 collective-permute-start.3
  3.3 2.6 %collective-permute-start = (bf16[2816,128]{1,0:T(8,128)(2,1)}, bf16[2816,128]{1,0:T(8,128)(2,1)S(1)}, u32[]{:S(2)}, u32[]{:S(2)}) collective-permute-start(bf16[2816,128]{1,0:T(8,128)(2,1)} %get-tuple-element.42.refs_0_), channel_id=1, source_target_pairs={{0,4},{2,6},{4,0},{6,2},{8,12},{10,14},{12,8},{14,10},{1,5},{3,7},... | collective-permute-start | bytes 2162696 | tf_op jit(solution)/shard_map/ppermute | solution.py:201
  5.9 2.6 %collective-permute-start.1 = (bf16[2816,128]{1,0:T(8,128)(2,1)}, bf16[2816,128]{1,0:T(8,128)(2,1)S(1)}, u32[]{:S(2)}, u32[]{:S(2)}) collective-permute-start(bf16[2816,128]{1,0:T(8,128)(2,1)} %get-tuple-element.42.refs_0_), channel_id=1, source_target_pairs={{0,8},{2,10},{4,12},{6,14},{8,0},{10,2},{12,4},{14,6},{1,9},{3,11}... | collective-permute-start | bytes 2162696 | tf_op jit(solution)/shard_map/ppermute | solution.py:201
  8.5 1.5 %collective-permute-start.2 = (bf16[2816,128]{1,0:T(8,128)(2,1)}, bf16[2816,128]{1,0:T(8,128)(2,1)S(1)}, u32[]{:S(2)}, u32[]{:S(2)}) collective-permute-start(bf16[2816,128]{1,0:T(8,128)(2,1)} %get-tuple-element.42.refs_0_), channel_id=1, source_target_pairs={{0,2},{2,0},{4,6},{6,4},{8,10},{10,8},{12,14},{14,12},{1,3},{3,1},... | collective-permute-start | bytes 2162696 | tf_op jit(solution)/shard_map/ppermute | solution.py:201
  10.0 0.5 collective-permute-start.4
  10.5 1.2 copy-done.2
  11.7 0.7 copy-done.3
  12.4 3.4 %shard_map.56 = f32[2,1024]{1,0:T(2,128)S(1)} custom-call(s32[1,1024]{1,0:T(1,128)S(1)} %bitcast.23, f32[1024,2,128]{2,1,0:T(2,128)S(1)} %bitcast.22), custom_call_target="tpu_custom_call" | custom-call | flops 1610612736 | bytes 1048576 | tf_op jit(solution)/shard_map/pallas_call | solution.py:71
  16.2 0.5 collective-permute-start.7
  16.7 21.7 %collective-permute-done.refs_0_ = bf16[2816,128]{1,0:T(8,128)(2,1)S(1)} collective-permute-done((bf16[2816,128]{1,0:T(8,128)(2,1)}, bf16[2816,128]{1,0:T(8,128)(2,1)S(1)}, u32[]{:S(2)}, u32[]{:S(2)}) %collective-permute-start) | collective-permute-done | bytes 720928 | tf_op jit(solution)/shard_map/ppermute | solution.py:201
  38.4 1.1 collective-permute-start.8
  39.4 1.1 collective-permute-done.1.refs_2_
  40.6 1.7 %collective-permute-done.4.refs_3_ = bf16[2816,128]{1,0:T(8,128)(2,1)} collective-permute-done((bf16[2816,128]{1,0:T(8,128)(2,1)S(1)}, bf16[2816,128]{1,0:T(8,128)(2,1)}, u32[]{:S(2)}, u32[]{:S(2)}) %collective-permute-start.4) | collective-permute-done | bytes 720928 | tf_op jit(solution)/shard_map/ppermute | solution.py:201
  42.2 1.5 %collective-permute-start.10 = (bf16[2816,128]{1,0:T(8,128)(2,1)S(1)}, bf16[2816,128]{1,0:T(8,128)(2,1)S(1)}, u32[]{:S(2)}, u32[]{:S(2)}) collective-permute-start(bf16[2816,128]{1,0:T(8,128)(2,1)S(1)} %collective-permute-done.1.refs_2_), channel_id=1, source_target_pairs={{0,2},{2,0},{4,6},{6,4},{8,10},{10,8},{12,14},{14,12},{1,3},{3,1},... | collective-permute-start | bytes 2162696 | tf_op jit(solution)/shard_map/ppermute | solution.py:201
  43.7 0.5 collective-permute-start.9
  44.3 0.5 collective-permute-start.5
  44.9 1.1 copy-done.1
  46.0 3.4 %shard_map.57 = (f32[16,2,256,256]{3,2,1,0:T(8,128)S(1)}, f32[8,128]{1,0:T(8,128)S(1)}) custom-call(s32[16]{0:T(128)S(1)} %get-tuple-element.84.rows_ref, s32[16]{0:T(128)S(1)} %get-tuple-element.83.cols_ref, s32[16]{0:T(128)S(1)} %fusion.1.valid_ref, s32[2]{0:T(128)S(1)} %pad_add_fusion.at_ref, bf16[2816,128]{1,0:T(8,128)(2,1)S(1)} %copy-done.1, ...), custom_call_target="tpu_custom_call" | custom-call | flops 1000 | bytes 1000 | tf_op jit(solution)/shard_map/pallas_call | solution.py:175
  49.4 3.4 %copy-done = f32[16,2,256,256]{3,2,1,0:T(8,128)S(1)} copy-done((f32[16,2,256,256]{3,2,1,0:T(8,128)S(1)}, f32[16,2,256,256]{3,2,1,0:T(8,128)}, u32[]{:S(2)}) %copy-start) | copy-done | bytes 8388632
  52.7 3.8 %shard_map.58 = (f32[16,2,256,256]{3,2,1,0:T(8,128)S(1)}, f32[8,128]{1,0:T(8,128)S(1)}) custom-call(s32[16]{0:T(128)S(1)} %get-tuple-element.86.rows_ref, s32[16]{0:T(128)S(1)} %get-tuple-element.85.cols_ref, s32[16]{0:T(128)S(1)} %fusion.valid_ref, s32[2]{0:T(128)S(1)} %pad_add_fusion.at_ref, bf16[2816,128]{1,0:T(8,128)(2,1)S(1)} %copy-done.1, ...), custom_call_target="tpu_custom_call" | custom-call | flops 1000 | bytes 1000 | tf_op jit(solution)/shard_map/pallas_call | solution.py:175
  56.6 11.7 %collective-permute-done.7.refs_1_ = bf16[2816,128]{1,0:T(8,128)(2,1)S(1)} collective-permute-done((bf16[2816,128]{1,0:T(8,128)(2,1)S(1)}, bf16[2816,128]{1,0:T(8,128)(2,1)S(1)}, u32[]{:S(2)}, u32[]{:S(2)}) %collective-permute-start.7) | collective-permute-done | bytes 720928 | tf_op jit(solution)/shard_map/ppermute | solution.py:201
  68.3 4.5 %collective-permute-done.8.refs_3_ = bf16[2816,128]{1,0:T(8,128)(2,1)S(1)} collective-permute-done((bf16[2816,128]{1,0:T(8,128)(2,1)S(1)}, bf16[2816,128]{1,0:T(8,128)(2,1)S(1)}, u32[]{:S(2)}, u32[]{:S(2)}) %collective-permute-start.8) | collective-permute-done | bytes 720928 | tf_op jit(solution)/shard_map/ppermute | solution.py:201
  72.8 2.0 %collective-permute-done.9.refs_2_ = bf16[2816,128]{1,0:T(8,128)(2,1)S(1)} collective-permute-done((bf16[2816,128]{1,0:T(8,128)(2,1)S(1)}, bf16[2816,128]{1,0:T(8,128)(2,1)S(1)}, u32[]{:S(2)}, u32[]{:S(2)}) %collective-permute-start.9) | collective-permute-done | bytes 720928 | tf_op jit(solution)/shard_map/ppermute | solution.py:201
  74.8 1.5 %collective-permute-start.11 = (bf16[2816,128]{1,0:T(8,128)(2,1)S(1)}, bf16[2816,128]{1,0:T(8,128)(2,1)S(1)}, u32[]{:S(2)}, u32[]{:S(2)}) collective-permute-start(bf16[2816,128]{1,0:T(8,128)(2,1)S(1)} %collective-permute-done.8.refs_3_), channel_id=1, source_target_pairs={{0,2},{2,0},{4,6},{6,4},{8,10},{10,8},{12,14},{14,12},{1,3},{3,1},... | collective-permute-start | bytes 2162696 | tf_op jit(solution)/shard_map/ppermute | solution.py:201
  76.3 0.4 collective-permute-start.13
  76.7 0.5 collective-permute-start.14
  77.3 7.6 %collective-permute-done.5.refs_0_ = bf16[2816,128]{1,0:T(8,128)(2,1)S(1)} collective-permute-done((bf16[2816,128]{1,0:T(8,128)(2,1)S(1)}, bf16[2816,128]{1,0:T(8,128)(2,1)S(1)}, u32[]{:S(2)}, u32[]{:S(2)}) %collective-permute-start.5) | collective-permute-done | bytes 720928 | tf_op jit(solution)/shard_map/ppermute | solution.py:201
  84.9 1.9 %collective-permute-start.6 = (bf16[2816,128]{1,0:T(8,128)(2,1)S(1)}, bf16[2816,128]{1,0:T(8,128)(2,1)S(1)}, u32[]{:S(2)}, u32[]{:S(2)}) collective-permute-start(bf16[2816,128]{1,0:T(8,128)(2,1)S(1)} %collective-permute-done.5.refs_0_), channel_id=1, source_target_pairs={{0,2},{2,0},{4,6},{6,4},{8,10},{10,8},{12,14},{14,12},{1,3},{3,1},... | collective-permute-start | bytes 2162696 | tf_op jit(solution)/shard_map/ppermute | solution.py:201
  86.7 7.1 %collective-permute-done.11.refs_5_ = bf16[2816,128]{1,0:T(8,128)(2,1)S(1)} collective-permute-done((bf16[2816,128]{1,0:T(8,128)(2,1)S(1)}, bf16[2816,128]{1,0:T(8,128)(2,1)S(1)}, u32[]{:S(2)}, u32[]{:S(2)}) %collective-permute-start.11) | collective-permute-done | bytes 720928 | tf_op jit(solution)/shard_map/ppermute | solution.py:201
  93.9 0.4 collective-permute-start.12
  94.3 4.7 %shard_map.59 = (f32[16,2,256,256]{3,2,1,0:T(8,128)S(1)}, f32[8,128]{1,0:T(8,128)S(1)}) custom-call(s32[16]{0:T(128)S(1)} %get-tuple-element.84.rows_ref, s32[16]{0:T(128)S(1)} %get-tuple-element.83.cols_ref, s32[16]{0:T(128)S(1)} %fusion.1.valid_ref, s32[2]{0:T(128)S(1)} %pad_add_fusion.at_ref, ...), custom_call_target="tpu_custom_call", output_to_operand_aliasing={{0}: (11, {})} | custom-call | flops 1000 | bytes 1000 | tf_op jit(solution)/shard_map/pallas_call | solution.py:175
  99.0 4.7 %shard_map.60 = (f32[16,2,256,256]{3,2,1,0:T(8,128)S(1)}, f32[8,128]{1,0:T(8,128)S(1)}) custom-call(s32[16]{0:T(128)S(1)} %get-tuple-element.86.rows_ref, s32[16]{0:T(128)S(1)} %get-tuple-element.85.cols_ref, s32[16]{0:T(128)S(1)} %fusion.valid_ref, s32[2]{0:T(128)S(1)} %pad_add_fusion.at_ref, ...), custom_call_target="tpu_custom_call", output_to_operand_aliasing={{0}: (11, {})} | custom-call | flops 1000 | bytes 1000 | tf_op jit(solution)/shard_map/pallas_call | solution.py:175
  103.7 5.6 %collective-permute-done.14.refs_3_ = bf16[2816,128]{1,0:T(8,128)(2,1)S(1)} collective-permute-done((bf16[2816,128]{1,0:T(8,128)(2,1)S(1)}, bf16[2816,128]{1,0:T(8,128)(2,1)S(1)}, u32[]{:S(2)}, u32[]{:S(2)}) %collective-permute-start.14) | collective-permute-done | bytes 720928 | tf_op jit(solution)/shard_map/ppermute | solution.py:201
  109.3 4.0 %shard_map.61 = (f32[16,2,256,256]{3,2,1,0:T(8,128)S(1)}, f32[8,128]{1,0:T(8,128)S(1)}) custom-call(s32[16]{0:T(128)S(1)} %get-tuple-element.86.rows_ref, s32[16]{0:T(128)S(1)} %get-tuple-element.85.cols_ref, s32[16]{0:T(128)S(1)} %fusion.valid_ref, s32[2]{0:T(128)S(1)} %pad_add_fusion.at_ref, ...), custom_call_target="tpu_custom_call", output_to_operand_aliasing={{0}: (9, {})} | custom-call | flops 1000 | bytes 1000 | tf_op jit(solution)/shard_map/pallas_call | solution.py:175
  113.3 3.4 %shard_map.62 = (bf16[2,2,256,256]{3,2,1,0:T(8,128)(2,1)S(1)}, bf16[2,2,256,256]{3,2,1,0:T(8,128)(2,1)S(1)}, bf16[2,2,256,256]{3,2,1,0:T(8,128)(2,1)S(1)}, bf16[...) custom-call(s32[16]{0:T(128)S(1)} %get-tuple-element.84.rows_ref, ...), custom_call_target="tpu_custom_call" | custom-call | flops 1000 | bytes 1000 | tf_op jit(solution)/shard_map/pallas_call | solution.py:175
  116.8 0.5 collective-permute-start.18
  117.4 4.5 %collective-permute-done.6.refs_0_ = bf16[2816,128]{1,0:T(8,128)(2,1)S(1)} collective-permute-done((bf16[2816,128]{1,0:T(8,128)(2,1)S(1)}, bf16[2816,128]{1,0:T(8,128)(2,1)S(1)}, u32[]{:S(2)}, u32[]{:S(2)}) %collective-permute-start.6) | collective-permute-done | bytes 720928 | tf_op jit(solution)/shard_map/ppermute | solution.py:201
  121.9 0.5 collective-permute-start.21
  122.5 0.4 collective-permute-start.16
  123.0 0.8 collective-permute-done.20.refs_9_
  123.8 0.1 collective-permute-start.23
  124.0 0.6 collective-permute-done.21.refs_10_
  124.6 0.1 collective-permute-start.24
  124.7 2.7 %collective-permute-done.22.refs_11_ = bf16[2,2,256,256]{3,2,1,0:T(8,128)(2,1)S(1)} collective-permute-done((bf16[2,2,256,256]{3,2,1,0:T(8,128)(2,1)S(1)}, bf16[2,2,256,256]{3,2,1,0:T(8,128)(2,1)S(1)}, u32[]{:S(2)}, u32[]{:S(2)}) %collective-permute-start.22) | collective-permute-done | bytes 524320 | tf_op jit(solution)/shard_map/ppermute | solution.py:204
  127.4 0.7 collective-permute-done.23.refs_12_
  128.1 0.7 collective-permute-done.24.refs_13_
  128.9 4.9 %shard_map.63 = f32[16,2,256,256]{3,2,1,0:T(8,128)} custom-call(s32[16]{0:T(128)S(1)} %get-tuple-element.86.rows_ref, s32[16]{0:T(128)S(1)} %get-tuple-element.85.cols_ref, s32[16]{0:T(128)S(1)} %fusion.valid_ref, s32[2]{0:T(128)S(1)} %pad_add_fusion.at_ref, bf16[2816,128]{1,0:T(8,128)(2,1)S(1)} %collective-permute-done.6.refs_0_, ...), custom_call_target="tpu_custom_call" | custom-call | flops 1000 | bytes 1000 | tf_op jit(solution)/shard_map/pallas_call | solution.py:175
  (34 shorter events, 0.7 us)
Async XLA Ops:
  0.0 16.0 %copy-start.4 = (s32[256,2]{0,1:T(2,128)S(1)}, s32[256,2]{0,1:T(2,128)}, u32[]{:S(2)}) copy-start(s32[256,2]{0,1:T(2,128)} %param.8) | copy-start | bytes 6148
  2.8 7.1 %collective-permute-start.3 = (bf16[2816,128]{1,0:T(8,128)(2,1)}, bf16[2816,128]{1,0:T(8,128)(2,1)S(1)}, u32[]{:S(2)}, u32[]{:S(2)}) collective-permute-start(bf16[2816,128]{1,0:T(8,128)(2,1)} %get-tuple-element.43), channel_id=1, source_target_pairs={{0,1},{1,0},{2,3},{3,2},{4,5},{5,4},{6,7},{7,6},{8,9},{9,8},{10,11... | collective-permute-start | bytes 2162696 | tf_op jit(solution)/shard_map/ppermute | solution.py:204
  3.3 35.1 %collective-permute-start = (bf16[2816,128]{1,0:T(8,128)(2,1)}, bf16[2816,128]{1,0:T(8,128)(2,1)S(1)}, u32[]{:S(2)}, u32[]{:S(2)}) collective-permute-start(bf16[2816,128]{1,0:T(8,128)(2,1)} %get-tuple-element.42.refs_0_), channel_id=1, source_target_pairs={{0,4},{2,6},{4,0},{6,2},{8,12},{10,14},{12,8},{14,10},{1,5},{3,7},... | collective-permute-start | bytes 2162696 | tf_op jit(solution)/shard_map/ppermute | solution.py:201
  5.9 34.7 %collective-permute-start.1 = (bf16[2816,128]{1,0:T(8,128)(2,1)}, bf16[2816,128]{1,0:T(8,128)(2,1)S(1)}, u32[]{:S(2)}, u32[]{:S(2)}) collective-permute-start(bf16[2816,128]{1,0:T(8,128)(2,1)} %get-tuple-element.42.refs_0_), channel_id=1, source_target_pairs={{0,8},{2,10},{4,12},{6,14},{8,0},{10,2},{12,4},{14,6},{1,9},{3,11}... | collective-permute-start | bytes 2162696 | tf_op jit(solution)/shard_map/ppermute | solution.py:201
  8.5 32.1 %collective-permute-start.2 = (bf16[2816,128]{1,0:T(8,128)(2,1)}, bf16[2816,128]{1,0:T(8,128)(2,1)S(1)}, u32[]{:S(2)}, u32[]{:S(2)}) collective-permute-start(bf16[2816,128]{1,0:T(8,128)(2,1)} %get-tuple-element.42.refs_0_), channel_id=1, source_target_pairs={{0,2},{2,0},{4,6},{6,4},{8,10},{10,8},{12,14},{14,12},{1,3},{3,1},... | collective-permute-start | bytes 2162696 | tf_op jit(solution)/shard_map/ppermute | solution.py:201
  10.0 32.3 %collective-permute-start.4 = (bf16[2816,128]{1,0:T(8,128)(2,1)S(1)}, bf16[2816,128]{1,0:T(8,128)(2,1)}, u32[]{:S(2)}, u32[]{:S(2)}) collective-permute-start(bf16[2816,128]{1,0:T(8,128)(2,1)S(1)} %collective-permute-done.3.refs_1_), channel_id=1, source_target_pairs={{0,2},{2,0},{4,6},{6,4},{8,10},{10,8},{12,14},{14,12},{1,3},{3,1},... | collective-permute-start | bytes 2162696 | tf_op jit(solution)/shard_map/ppermute | solution.py:201
  10.5 1.2 copy-start.2
  11.7 0.7 copy-start.3
  16.2 52.1 %collective-permute-start.7 = (bf16[2816,128]{1,0:T(8,128)(2,1)S(1)}, bf16[2816,128]{1,0:T(8,128)(2,1)S(1)}, u32[]{:S(2)}, u32[]{:S(2)}) collective-permute-start(bf16[2816,128]{1,0:T(8,128)(2,1)S(1)} %collective-permute-done.3.refs_1_), channel_id=1, source_target_pairs={{0,4},{2,6},{4,0},{6,2},{8,12},{10,14},{12,8},{14,10},{1,5},{3,7},... | collective-permute-start | bytes 2162696 | tf_op jit(solution)/shard_map/ppermute | solution.py:201
  38.4 34.4 %collective-permute-start.8 = (bf16[2816,128]{1,0:T(8,128)(2,1)S(1)}, bf16[2816,128]{1,0:T(8,128)(2,1)S(1)}, u32[]{:S(2)}, u32[]{:S(2)}) collective-permute-start(bf16[2816,128]{1,0:T(8,128)(2,1)S(1)} %collective-permute-done.3.refs_1_), channel_id=1, source_target_pairs={{0,8},{2,10},{4,12},{6,14},{8,0},{10,2},{12,4},{14,6},{1,9},{3,11}... | collective-permute-start | bytes 2162696 | tf_op jit(solution)/shard_map/ppermute | solution.py:201
  42.2 30.6 %collective-permute-start.10 = (bf16[2816,128]{1,0:T(8,128)(2,1)S(1)}, bf16[2816,128]{1,0:T(8,128)(2,1)S(1)}, u32[]{:S(2)}, u32[]{:S(2)}) collective-permute-start(bf16[2816,128]{1,0:T(8,128)(2,1)S(1)} %collective-permute-done.1.refs_2_), channel_id=1, source_target_pairs={{0,2},{2,0},{4,6},{6,4},{8,10},{10,8},{12,14},{14,12},{1,3},{3,1},... | collective-permute-start | bytes 2162696 | tf_op jit(solution)/shard_map/ppermute | solution.py:201
  43.7 31.1 %collective-permute-start.9 = (bf16[2816,128]{1,0:T(8,128)(2,1)S(1)}, bf16[2816,128]{1,0:T(8,128)(2,1)S(1)}, u32[]{:S(2)}, u32[]{:S(2)}) collective-permute-start(bf16[2816,128]{1,0:T(8,128)(2,1)S(1)} %collective-permute-done.refs_0_), channel_id=1, source_target_pairs={{0,2},{2,0},{4,6},{6,4},{8,10},{10,8},{12,14},{14,12},{1,3},{3,1},... | collective-permute-start | bytes 2162696 | tf_op jit(solution)/shard_map/ppermute | solution.py:201
  44.3 40.5 %collective-permute-start.5 = (bf16[2816,128]{1,0:T(8,128)(2,1)S(1)}, bf16[2816,128]{1,0:T(8,128)(2,1)S(1)}, u32[]{:S(2)}, u32[]{:S(2)}) collective-permute-start(bf16[2816,128]{1,0:T(8,128)(2,1)S(1)} %collective-permute-done.1.refs_2_), channel_id=1, source_target_pairs={{0,4},{2,6},{4,0},{6,2},{8,12},{10,14},{12,8},{14,10},{1,5},{3,7},... | collective-permute-start | bytes 2162696 | tf_op jit(solution)/shard_map/ppermute | solution.py:201
  44.9 1.1 copy-start.1
  49.4 3.4 %copy-start = (f32[16,2,256,256]{3,2,1,0:T(8,128)S(1)}, f32[16,2,256,256]{3,2,1,0:T(8,128)}, u32[]{:S(2)}) copy-start(f32[16,2,256,256]{3,2,1,0:T(8,128)} %refs_5_.1) | copy-start | bytes 25165828
  74.8 19.1 %collective-permute-start.11 = (bf16[2816,128]{1,0:T(8,128)(2,1)S(1)}, bf16[2816,128]{1,0:T(8,128)(2,1)S(1)}, u32[]{:S(2)}, u32[]{:S(2)}) collective-permute-start(bf16[2816,128]{1,0:T(8,128)(2,1)S(1)} %collective-permute-done.8.refs_3_), channel_id=1, source_target_pairs={{0,2},{2,0},{4,6},{6,4},{8,10},{10,8},{12,14},{14,12},{1,3},{3,1},... | collective-permute-start | bytes 2162696 | tf_op jit(solution)/shard_map/ppermute | solution.py:201
  76.3 27.4 %collective-permute-start.13 = (bf16[2816,128]{1,0:T(8,128)(2,1)S(1)}, bf16[2816,128]{1,0:T(8,128)(2,1)S(1)}, u32[]{:S(2)}, u32[]{:S(2)}) collective-permute-start(bf16[2816,128]{1,0:T(8,128)(2,1)S(1)} %collective-permute-done.8.refs_3_), channel_id=1, source_target_pairs={{0,4},{2,6},{4,0},{6,2},{8,12},{10,14},{12,8},{14,10},{1,5},{3,7},... | collective-permute-start | bytes 2162696 | tf_op jit(solution)/shard_map/ppermute | solution.py:201
  76.7 32.6 %collective-permute-start.14 = (bf16[2816,128]{1,0:T(8,128)(2,1)S(1)}, bf16[2816,128]{1,0:T(8,128)(2,1)S(1)}, u32[]{:S(2)}, u32[]{:S(2)}) collective-permute-start(bf16[2816,128]{1,0:T(8,128)(2,1)S(1)} %collective-permute-done.7.refs_1_), channel_id=1, source_target_pairs={{0,2},{2,0},{4,6},{6,4},{8,10},{10,8},{12,14},{14,12},{1,3},{3,1},... | collective-permute-start | bytes 2162696 | tf_op jit(solution)/shard_map/ppermute | solution.py:201
  84.9 37.0 %collective-permute-start.6 = (bf16[2816,128]{1,0:T(8,128)(2,1)S(1)}, bf16[2816,128]{1,0:T(8,128)(2,1)S(1)}, u32[]{:S(2)}, u32[]{:S(2)}) collective-permute-start(bf16[2816,128]{1,0:T(8,128)(2,1)S(1)} %collective-permute-done.5.refs_0_), channel_id=1, source_target_pairs={{0,2},{2,0},{4,6},{6,4},{8,10},{10,8},{12,14},{14,12},{1,3},{3,1},... | collective-permute-start | bytes 2162696 | tf_op jit(solution)/shard_map/ppermute | solution.py:201
  93.9 28.0 %collective-permute-start.12 = (bf16[2816,128]{1,0:T(8,128)(2,1)S(1)}, bf16[2816,128]{1,0:T(8,128)(2,1)S(1)}, u32[]{:S(2)}, u32[]{:S(2)}) collective-permute-start(bf16[2816,128]{1,0:T(8,128)(2,1)S(1)} %collective-permute-done.11.refs_5_), channel_id=1, source_target_pairs={{0,4},{2,6},{4,0},{6,2},{8,12},{10,14},{12,8},{14,10},{1,5},{3,7},... | collective-permute-start | bytes 2162696 | tf_op jit(solution)/shard_map/ppermute | solution.py:201
  116.8 5.7 %collective-permute-start.17 = (bf16[2,2,256,256]{3,2,1,0:T(8,128)(2,1)S(1)}, bf16[2,2,256,256]{3,2,1,0:T(8,128)(2,1)S(1)}, u32[]{:S(2)}, u32[]{:S(2)}) collective-permute-start(bf16[2,2,256,256]{3,2,1,0:T(8,128)(2,1)S(1)} %get-tuple-element.70), channel_id=1, source_target_pairs={{0,1},{1,0},{2,3},{3,2},{4,5},{5,4},{6,7},{7,6},{8,9},{9,8},{10,11... | collective-permute-start | bytes 1572872 | tf_op jit(solution)/shard_map/ppermute | solution.py:204
  116.8 5.7 %collective-permute-start.18 = (bf16[2,2,256,256]{3,2,1,0:T(8,128)(2,1)S(1)}, bf16[2,2,256,256]{3,2,1,0:T(8,128)(2,1)S(1)}, u32[]{:S(2)}, u32[]{:S(2)}) collective-permute-start(bf16[2,2,256,256]{3,2,1,0:T(8,128)(2,1)S(1)} %get-tuple-element.71), channel_id=1, source_target_pairs={{0,1},{1,0},{2,3},{3,2},{4,5},{5,4},{6,7},{7,6},{8,9},{9,8},{10,11... | collective-permute-start | bytes 1572872 | tf_op jit(solution)/shard_map/ppermute | solution.py:204
  117.3 5.6 %collective-permute-start.19 = (bf16[2,2,256,256]{3,2,1,0:T(8,128)(2,1)S(1)}, bf16[2,2,256,256]{3,2,1,0:T(8,128)(2,1)S(1)}, u32[]{:S(2)}, u32[]{:S(2)}) collective-permute-start(bf16[2,2,256,256]{3,2,1,0:T(8,128)(2,1)S(1)} %get-tuple-element.72), channel_id=1, source_target_pairs={{0,1},{1,0},{2,3},{3,2},{4,5},{5,4},{6,7},{7,6},{8,9},{9,8},{10,11... | collective-permute-start | bytes 1572872 | tf_op jit(solution)/shard_map/ppermute | solution.py:204
  121.9 1.9 %collective-permute-start.20 = (bf16[2,2,256,256]{3,2,1,0:T(8,128)(2,1)S(1)}, bf16[2,2,256,256]{3,2,1,0:T(8,128)(2,1)S(1)}, u32[]{:S(2)}, u32[]{:S(2)}) collective-permute-start(bf16[2,2,256,256]{3,2,1,0:T(8,128)(2,1)S(1)} %get-tuple-element.73), channel_id=1, source_target_pairs={{0,1},{1,0},{2,3},{3,2},{4,5},{5,4},{6,7},{7,6},{8,9},{9,8},{10,11... | collective-permute-start | bytes 1572872 | tf_op jit(solution)/shard_map/ppermute | solution.py:204
  121.9 2.7 %collective-permute-start.21 = (bf16[2,2,256,256]{3,2,1,0:T(8,128)(2,1)S(1)}, bf16[2,2,256,256]{3,2,1,0:T(8,128)(2,1)S(1)}, u32[]{:S(2)}, u32[]{:S(2)}) collective-permute-start(bf16[2,2,256,256]{3,2,1,0:T(8,128)(2,1)S(1)} %get-tuple-element.74), channel_id=1, source_target_pairs={{0,1},{1,0},{2,3},{3,2},{4,5},{5,4},{6,7},{7,6},{8,9},{9,8},{10,11... | collective-permute-start | bytes 1572872 | tf_op jit(solution)/shard_map/ppermute | solution.py:204
  122.4 6.5 %collective-permute-start.15 = (bf16[2816,128]{1,0:T(8,128)(2,1)S(1)}, bf16[2816,128]{1,0:T(8,128)(2,1)S(1)}, u32[]{:S(2)}, u32[]{:S(2)}) collective-permute-start(bf16[2816,128]{1,0:T(8,128)(2,1)S(1)} %collective-permute-done.12.refs_1_), channel_id=1, source_target_pairs={{0,1},{1,0},{2,3},{3,2},{4,5},{5,4},{6,7},{7,6},{8,9},{9,8},{10,11... | collective-permute-start | bytes 2162696 | tf_op jit(solution)/shard_map/ppermute | solution.py:204
  122.5 6.4 %collective-permute-start.16 = (bf16[2816,128]{1,0:T(8,128)(2,1)S(1)}, bf16[2816,128]{1,0:T(8,128)(2,1)S(1)}, u32[]{:S(2)}, u32[]{:S(2)}) collective-permute-start(bf16[2816,128]{1,0:T(8,128)(2,1)S(1)} %collective-permute-done.6.refs_0_), channel_id=1, source_target_pairs={{0,1},{1,0},{2,3},{3,2},{4,5},{5,4},{6,7},{7,6},{8,9},{9,8},{10,11... | collective-permute-start | bytes 2162696 | tf_op jit(solution)/shard_map/ppermute | solution.py:204
  122.9 4.4 %collective-permute-start.22 = (bf16[2,2,256,256]{3,2,1,0:T(8,128)(2,1)S(1)}, bf16[2,2,256,256]{3,2,1,0:T(8,128)(2,1)S(1)}, u32[]{:S(2)}, u32[]{:S(2)}) collective-permute-start(bf16[2,2,256,256]{3,2,1,0:T(8,128)(2,1)S(1)} %get-tuple-element.75), channel_id=1, source_target_pairs={{0,1},{1,0},{2,3},{3,2},{4,5},{5,4},{6,7},{7,6},{8,9},{9,8},{10,11... | collective-permute-start | bytes 1572872 | tf_op jit(solution)/shard_map/ppermute | solution.py:204
  123.8 4.3 %collective-permute-start.23 = (bf16[2,2,256,256]{3,2,1,0:T(8,128)(2,1)S(1)}, bf16[2,2,256,256]{3,2,1,0:T(8,128)(2,1)S(1)}, u32[]{:S(2)}, u32[]{:S(2)}) collective-permute-start(bf16[2,2,256,256]{3,2,1,0:T(8,128)(2,1)S(1)} %get-tuple-element.76), channel_id=1, source_target_pairs={{0,1},{1,0},{2,3},{3,2},{4,5},{5,4},{6,7},{7,6},{8,9},{9,8},{10,11... | collective-permute-start | bytes 1572872 | tf_op jit(solution)/shard_map/ppermute | solution.py:204
  124.6 4.3 %collective-permute-start.24 = (bf16[2,2,256,256]{3,2,1,0:T(8,128)(2,1)S(1)}, bf16[2,2,256,256]{3,2,1,0:T(8,128)(2,1)S(1)}, u32[]{:S(2)}, u32[]{:S(2)}) collective-permute-start(bf16[2,2,256,256]{3,2,1,0:T(8,128)(2,1)S(1)} %get-tuple-element.77), channel_id=1, source_target_pairs={{0,1},{1,0},{2,3},{3,2},{4,5},{5,4},{6,7},{7,6},{8,9},{9,8},{10,11... | collective-permute-start | bytes 1572872 | tf_op jit(solution)/shard_map/ppermute | solution.py:204

commit v4 on v3

--- a/solution.py
+++ b/solution.py
@@ -8,6 +8,7 @@
 from jax.sharding import PartitionSpec as P
 
 LANES = 128
+GROUPS = (2, 2, 2, 1, 1)
 COST = 1000
 LIMIT = 16
 GROUP = 2
@@ -79,7 +80,11 @@
     )(stations[None, :], table)
 
 
-def tiles_kernel(places, form, unroll, rows_ref, cols_ref, valid_ref, at_ref, *refs):
+def groups_of(count):
+    return GROUPS if count == sum(GROUPS) else (1,) * count
+
+
+def tiles_kernel(places, form, unroll, first_got, rows_ref, cols_ref, valid_ref, at_ref, *refs):
     n = len(places)
     pieces = refs[: 2 * n]
     weight_ref = refs[2 * n]
@@ -90,9 +95,11 @@
         _, out_ref, token_ref = refs
     elif form == "last":
         acc_ref, *got_refs, _, result_ref, out_ref, sem = refs
-    else:
+    elif form == "give":
         acc_ref, _, *outs, token_ref = refs
         out_ref = outs[0]
+    else:
+        acc_ref, *got_refs, _, out_ref, token_ref = refs
     if form != "last":
         token_ref[...] = jnp.zeros_like(token_ref)
     slots = rows_ref.shape[0]
@@ -133,16 +140,19 @@
             value = both[part * side : (part + 1) * side]
             if acc_ref is not None:
                 value = acc_ref[slot, part] + value
-            if got_refs:
-                value = value + got_refs[i][step, part].astype(jnp.float32)
+            o, at = where[i]
+            if 0 <= o - first_got < len(got_refs):
+                value = value + got_refs[o - first_got][at * steps + step, part].astype(jnp.float32)
             if form == "give":
-                outs[i][step, part] = value.astype(out_ref.dtype)
+                o, at = where[i]
+                outs[o][at * steps + step, part] = value.astype(out_ref.dtype)
             else:
                 out_ref[slot, part] = value
         if form == "last":
             pltpu.make_async_copy(out_ref.at[slot], result_ref.at[slot], sem.at[slot]).start()
 
     steps = slots // unroll
+    where = [(o, at) for o, g in enumerate(groups_of(unroll)) for at in range(g)]
 
     group = unroll // 2 if form == "last" and unroll > 1 else unroll
     for base in range(0, unroll, group):
@@ -159,7 +169,7 @@
             pltpu.make_async_copy(out_ref.at[slot], result_ref.at[slot], sem.at[slot]).wait()
 
 
-def subtract(form, pieces, scalars, weights, shape, token, acc=None, got=()):
+def subtract(form, pieces, scalars, weights, shape, token, acc=None, got=(), first_got=0):
     n = len(pieces)
     places = [piece[:2] for piece in pieces]
     operands = [array for piece in pieces for array in piece[2:]] + [weights]
@@ -169,13 +179,13 @@
     unroll = 8 if shape[0] % 8 == 0 else 1
     result = jax.ShapeDtypeStruct(shape, jnp.float32)
     if form == "give":
-        result = [jax.ShapeDtypeStruct((shape[0] // unroll,) + shape[1:], jnp.bfloat16)] * unroll
+        result = [jax.ShapeDtypeStruct((shape[0] // unroll * g,) + shape[1:], jnp.bfloat16) for g in groups_of(unroll)]
     elif not last:
         result = pltpu.VMEM(shape, jnp.float32)
     return pl.pallas_call(
-        functools.partial(tiles_kernel, places, form, unroll),
+        functools.partial(tiles_kernel, places, form, unroll, first_got),
         in_specs=[pl.BlockSpec(memory_space=pltpu.SMEM)] * 4 + [vmem] * len(operands),
-        out_specs=ANY if last else [vmem] * (1 + (unroll if form == "give" else 1)),
+        out_specs=ANY if last else [vmem] * (1 + (len(result) if form == "give" else 1)),
         scratch_shapes=[pltpu.VMEM(shape, jnp.float32), pltpu.SemaphoreType.DMA((shape[0],))] if last else [],
         out_shape=result if last else [*(result if form == "give" else [result]), jax.ShapeDtypeStruct((8, LANES), jnp.float32)],
         input_output_aliases={4 + 2 * n + 1: 0} if form == "add" else {},
@@ -219,9 +229,9 @@
     X, Z1, Z2 = 1, 2, 4
     h0, give = turn(panel, rcv)
     h1 = swap(give)
-    A0 = send(h0, Z1)
     B0 = send(h0, Z2)
     X0 = send(h0, X)
+    A0 = send(h0, Z1)
     X1 = send(h1, X)
     A0, B0, X0, X1, weights = together((A0, B0, X0, X1, weights))
 
@@ -252,8 +262,8 @@
     XZZ0, ZXB1, token = together((XZZ0, ZXB1, token))
 
     far = X + Z1 + Z2
-    pieces = [(far, 0, XZZ0, ZXB1), (far, 1, swap(ZXB1), swap(XZZ0))]
-    return subtract("last", pieces, mine, weights, shape, token, home, got)
+    home, token = subtract("add", [(far, 0, XZZ0, ZXB1)], mine, weights, shape, token, home, got[:0])
+    return subtract("last", [(far, 1, swap(ZXB1), swap(XZZ0))], mine, weights, shape, token, home, got[0:], 0)
 
 
 def solution(mesh):

time: 134 us -> 133 us (level)
  waiting for transfers between devices: 73.2 us -> 69.7 us
  Pallas kernels: 35.1 us -> 37.6 us
    ppermute x11 -> x8, waiting for transfers between devices: 5.6 us -> 2.12 us  [swap(): return lax.ppermute(a, 'rcv', [(0, 1), (1, 0)])]
    pallas_call x7 -> x8, Pallas kernels: 28.9 us -> 31.4 us  [subtract(): pl.pallas_call(functools.partial(tiles_kernel, places, form, unroll, firs...]
  transfers between devices with their start and end apart: 25 -> 22, of which waited for: 15 -> 12; matrix products, arithmetic and copies ran while one was open for 0% -> 0% of each run, Pallas kernels for 20% -> 23%
where the time goes in v4:
time: 133 us
  waiting for transfers between devices  69.7 us (52%)
  Pallas kernels  37.6 us (28%)
  starting transfers between devices  18.2 us (14%)
  local copies, waits for them, and re-layouts  6.64 us (5%)
    ppermute x14, waiting for transfers between devices, send(): lax.ppermute(a, 'src', [(i, i ^ distance * span) for i in range(n_src)])  67.6 us
    pallas_call x8, Pallas kernels, subtract(): pl.pallas_call(functools.partial(tiles_kernel, places, form, unroll, firs...  31.4 us
    ppermute x14, starting transfers between devices, send(): lax.ppermute(a, 'src', [(i, i ^ distance * span) for i in range(n_src)])  16.1 us
    unnamed x10, local copies, waits for them, and re-layouts  6.4 us
    pallas_call x1, Pallas kernels, station_weights(): pl.pallas_call(weights_kernel, in_specs=[pl.BlockSpec(memory_space=pltpu....  3.43 us
    pallas_call x1, Pallas kernels, turn(): pl.pallas_call(turn_kernel, grid_spec=pltpu.PrefetchScalarGridSpec(num_sc...  2.83 us
  transfers between devices with their start and end apart: 22, of which 12 were waited for; matrix products, arithmetic and copies ran while one was open for 0% of the time, Pallas kernels for 23%

profile of v4, /device:TPU:0, one launch (start us, length us, event | category | flops | bytes accessed | tf_op | source)
XLA Modules:
  0.0 132.7 jit_solution(3184003785975417342)
XLA Ops:
  0.0 2.8 %shard_map.55 = (bf16[2816,128]{1,0:T(8,128)(2,1)}, bf16[2816,128]{1,0:T(8,128)(2,1)}) custom-call(s32[1]{0:T(128)} %bitcast.3._, f32[2,128,2816]{2,1,0:T(8,128)} %given_in.1, f32[2,128,2816]{2,1,0:T(8,128)} %given_in.1), custom_call_target="tpu_custom_call" | custom-call | bytes 4325376 | tf_op jit(solution)/shard_map/pallas_call | solution.py:30
  2.8 0.5 collective-permute-start.3
  3.3 2.6 %collective-permute-start = (bf16[2816,128]{1,0:T(8,128)(2,1)}, bf16[2816,128]{1,0:T(8,128)(2,1)S(1)}, u32[]{:S(2)}, u32[]{:S(2)}) collective-permute-start(bf16[2816,128]{1,0:T(8,128)(2,1)} %get-tuple-element.41.refs_0_), channel_id=1, source_target_pairs={{0,4},{2,6},{4,0},{6,2},{8,12},{10,14},{12,8},{14,10},{1,5},{3,7},... | collective-permute-start | bytes 2162696 | tf_op jit(solution)/shard_map/ppermute | solution.py:211
  5.9 2.6 %collective-permute-start.1 = (bf16[2816,128]{1,0:T(8,128)(2,1)}, bf16[2816,128]{1,0:T(8,128)(2,1)S(1)}, u32[]{:S(2)}, u32[]{:S(2)}) collective-permute-start(bf16[2816,128]{1,0:T(8,128)(2,1)} %get-tuple-element.41.refs_0_), channel_id=1, source_target_pairs={{0,8},{2,10},{4,12},{6,14},{8,0},{10,2},{12,4},{14,6},{1,9},{3,11}... | collective-permute-start | bytes 2162696 | tf_op jit(solution)/shard_map/ppermute | solution.py:211
  8.5 1.5 %collective-permute-start.2 = (bf16[2816,128]{1,0:T(8,128)(2,1)}, bf16[2816,128]{1,0:T(8,128)(2,1)S(1)}, u32[]{:S(2)}, u32[]{:S(2)}) collective-permute-start(bf16[2816,128]{1,0:T(8,128)(2,1)} %get-tuple-element.41.refs_0_), channel_id=1, source_target_pairs={{0,2},{2,0},{4,6},{6,4},{8,10},{10,8},{12,14},{14,12},{1,3},{3,1},... | collective-permute-start | bytes 2162696 | tf_op jit(solution)/shard_map/ppermute | solution.py:211
  10.0 0.5 collective-permute-start.4
  10.5 1.2 copy-done.2
  11.7 0.7 copy-done.3
  12.4 3.4 %shard_map.56 = f32[2,1024]{1,0:T(2,128)S(1)} custom-call(s32[1,1024]{1,0:T(1,128)S(1)} %bitcast.23, f32[1024,2,128]{2,1,0:T(2,128)S(1)} %bitcast.22), custom_call_target="tpu_custom_call" | custom-call | flops 1610612736 | bytes 1048576 | tf_op jit(solution)/shard_map/pallas_call | solution.py:72
  16.0 0.1 constant_dynamic-slice_fusion
  16.1 0.1 maximum_bitcast_fusion
  16.2 0.5 collective-permute-start.7
  16.7 21.7 %collective-permute-done.refs_0_ = bf16[2816,128]{1,0:T(8,128)(2,1)S(1)} collective-permute-done((bf16[2816,128]{1,0:T(8,128)(2,1)}, bf16[2816,128]{1,0:T(8,128)(2,1)S(1)}, u32[]{:S(2)}, u32[]{:S(2)}) %collective-permute-start) | collective-permute-done | bytes 720928 | tf_op jit(solution)/shard_map/ppermute | solution.py:211
  38.4 1.1 collective-permute-start.8
  39.4 1.1 collective-permute-done.1.refs_2_
  40.6 1.7 %collective-permute-done.4.refs_3_ = bf16[2816,128]{1,0:T(8,128)(2,1)} collective-permute-done((bf16[2816,128]{1,0:T(8,128)(2,1)S(1)}, bf16[2816,128]{1,0:T(8,128)(2,1)}, u32[]{:S(2)}, u32[]{:S(2)}) %collective-permute-start.4) | collective-permute-done | bytes 720928 | tf_op jit(solution)/shard_map/ppermute | solution.py:211
  42.2 1.5 %collective-permute-start.10 = (bf16[2816,128]{1,0:T(8,128)(2,1)S(1)}, bf16[2816,128]{1,0:T(8,128)(2,1)S(1)}, u32[]{:S(2)}, u32[]{:S(2)}) collective-permute-start(bf16[2816,128]{1,0:T(8,128)(2,1)S(1)} %collective-permute-done.1.refs_2_), channel_id=1, source_target_pairs={{0,2},{2,0},{4,6},{6,4},{8,10},{10,8},{12,14},{14,12},{1,3},{3,1},... | collective-permute-start | bytes 2162696 | tf_op jit(solution)/shard_map/ppermute | solution.py:211
  43.7 0.5 collective-permute-start.9
  44.2 0.1 pad_add_fusion.at_ref
  44.3 0.5 collective-permute-start.5
  44.9 1.1 copy-done.1
  46.0 3.4 %shard_map.57 = (f32[16,2,256,256]{3,2,1,0:T(8,128)S(1)}, f32[8,128]{1,0:T(8,128)S(1)}) custom-call(s32[16]{0:T(128)S(1)} %get-tuple-element.82.rows_ref, s32[16]{0:T(128)S(1)} %get-tuple-element.81.cols_ref, s32[16]{0:T(128)S(1)} %fusion.1.valid_ref, s32[2]{0:T(128)S(1)} %pad_add_fusion.at_ref, bf16[2816,128]{1,0:T(8,128)(2,1)S(1)} %copy-done.1, ...), custom_call_target="tpu_custom_call" | custom-call | flops 1000 | bytes 1000 | tf_op jit(solution)/shard_map/pallas_call | solution.py:185
  49.4 3.4 %copy-done = f32[16,2,256,256]{3,2,1,0:T(8,128)S(1)} copy-done((f32[16,2,256,256]{3,2,1,0:T(8,128)S(1)}, f32[16,2,256,256]{3,2,1,0:T(8,128)}, u32[]{:S(2)}) %copy-start) | copy-done | bytes 8388632
  52.7 3.8 %shard_map.58 = (f32[16,2,256,256]{3,2,1,0:T(8,128)S(1)}, f32[8,128]{1,0:T(8,128)S(1)}) custom-call(s32[16]{0:T(128)S(1)} %get-tuple-element.84.rows_ref, s32[16]{0:T(128)S(1)} %get-tuple-element.83.cols_ref, s32[16]{0:T(128)S(1)} %fusion.valid_ref, s32[2]{0:T(128)S(1)} %pad_add_fusion.at_ref, bf16[2816,128]{1,0:T(8,128)(2,1)S(1)} %copy-done.1, ...), custom_call_target="tpu_custom_call" | custom-call | flops 1000 | bytes 1000 | tf_op jit(solution)/shard_map/pallas_call | solution.py:185
  56.6 11.8 %collective-permute-done.7.refs_1_ = bf16[2816,128]{1,0:T(8,128)(2,1)S(1)} collective-permute-done((bf16[2816,128]{1,0:T(8,128)(2,1)S(1)}, bf16[2816,128]{1,0:T(8,128)(2,1)S(1)}, u32[]{:S(2)}, u32[]{:S(2)}) %collective-permute-start.7) | collective-permute-done | bytes 720928 | tf_op jit(solution)/shard_map/ppermute | solution.py:211
  68.3 4.5 %collective-permute-done.8.refs_3_ = bf16[2816,128]{1,0:T(8,128)(2,1)S(1)} collective-permute-done((bf16[2816,128]{1,0:T(8,128)(2,1)S(1)}, bf16[2816,128]{1,0:T(8,128)(2,1)S(1)}, u32[]{:S(2)}, u32[]{:S(2)}) %collective-permute-start.8) | collective-permute-done | bytes 720928 | tf_op jit(solution)/shard_map/ppermute | solution.py:211
  72.8 2.0 %collective-permute-done.9.refs_2_ = bf16[2816,128]{1,0:T(8,128)(2,1)S(1)} collective-permute-done((bf16[2816,128]{1,0:T(8,128)(2,1)S(1)}, bf16[2816,128]{1,0:T(8,128)(2,1)S(1)}, u32[]{:S(2)}, u32[]{:S(2)}) %collective-permute-start.9) | collective-permute-done | bytes 720928 | tf_op jit(solution)/shard_map/ppermute | solution.py:211
  74.8 1.5 %collective-permute-start.11 = (bf16[2816,128]{1,0:T(8,128)(2,1)S(1)}, bf16[2816,128]{1,0:T(8,128)(2,1)S(1)}, u32[]{:S(2)}, u32[]{:S(2)}) collective-permute-start(bf16[2816,128]{1,0:T(8,128)(2,1)S(1)} %collective-permute-done.8.refs_3_), channel_id=1, source_target_pairs={{0,2},{2,0},{4,6},{6,4},{8,10},{10,8},{12,14},{14,12},{1,3},{3,1},... | collective-permute-start | bytes 2162696 | tf_op jit(solution)/shard_map/ppermute | solution.py:211
  76.3 0.4 collective-permute-start.13
  76.7 0.5 collective-permute-start.14
  77.3 7.6 %collective-permute-done.5.refs_0_ = bf16[2816,128]{1,0:T(8,128)(2,1)S(1)} collective-permute-done((bf16[2816,128]{1,0:T(8,128)(2,1)S(1)}, bf16[2816,128]{1,0:T(8,128)(2,1)S(1)}, u32[]{:S(2)}, u32[]{:S(2)}) %collective-permute-start.5) | collective-permute-done | bytes 720928 | tf_op jit(solution)/shard_map/ppermute | solution.py:211
  84.9 1.9 %collective-permute-start.6 = (bf16[2816,128]{1,0:T(8,128)(2,1)S(1)}, bf16[2816,128]{1,0:T(8,128)(2,1)S(1)}, u32[]{:S(2)}, u32[]{:S(2)}) collective-permute-start(bf16[2816,128]{1,0:T(8,128)(2,1)S(1)} %collective-permute-done.5.refs_0_), channel_id=1, source_target_pairs={{0,2},{2,0},{4,6},{6,4},{8,10},{10,8},{12,14},{14,12},{1,3},{3,1},... | collective-permute-start | bytes 2162696 | tf_op jit(solution)/shard_map/ppermute | solution.py:211
  86.7 7.1 %collective-permute-done.11.refs_5_ = bf16[2816,128]{1,0:T(8,128)(2,1)S(1)} collective-permute-done((bf16[2816,128]{1,0:T(8,128)(2,1)S(1)}, bf16[2816,128]{1,0:T(8,128)(2,1)S(1)}, u32[]{:S(2)}, u32[]{:S(2)}) %collective-permute-start.11) | collective-permute-done | bytes 720928 | tf_op jit(solution)/shard_map/ppermute | solution.py:211
  93.9 0.4 collective-permute-start.12
  94.3 4.7 %shard_map.59 = (f32[16,2,256,256]{3,2,1,0:T(8,128)S(1)}, f32[8,128]{1,0:T(8,128)S(1)}) custom-call(s32[16]{0:T(128)S(1)} %get-tuple-element.82.rows_ref, s32[16]{0:T(128)S(1)} %get-tuple-element.81.cols_ref, s32[16]{0:T(128)S(1)} %fusion.1.valid_ref, s32[2]{0:T(128)S(1)} %pad_add_fusion.at_ref, ...), custom_call_target="tpu_custom_call", output_to_operand_aliasing={{0}: (11, {})} | custom-call | flops 1000 | bytes 1000 | tf_op jit(solution)/shard_map/pallas_call | solution.py:185
  99.0 4.7 %shard_map.60 = (f32[16,2,256,256]{3,2,1,0:T(8,128)S(1)}, f32[8,128]{1,0:T(8,128)S(1)}) custom-call(s32[16]{0:T(128)S(1)} %get-tuple-element.84.rows_ref, s32[16]{0:T(128)S(1)} %get-tuple-element.83.cols_ref, s32[16]{0:T(128)S(1)} %fusion.valid_ref, s32[2]{0:T(128)S(1)} %pad_add_fusion.at_ref, ...), custom_call_target="tpu_custom_call", output_to_operand_aliasing={{0}: (11, {})} | custom-call | flops 1000 | bytes 1000 | tf_op jit(solution)/shard_map/pallas_call | solution.py:185
  103.7 5.6 %collective-permute-done.14.refs_3_ = bf16[2816,128]{1,0:T(8,128)(2,1)S(1)} collective-permute-done((bf16[2816,128]{1,0:T(8,128)(2,1)S(1)}, bf16[2816,128]{1,0:T(8,128)(2,1)S(1)}, u32[]{:S(2)}, u32[]{:S(2)}) %collective-permute-start.14) | collective-permute-done | bytes 720928 | tf_op jit(solution)/shard_map/ppermute | solution.py:211
  109.3 4.0 %shard_map.61 = (f32[16,2,256,256]{3,2,1,0:T(8,128)S(1)}, f32[8,128]{1,0:T(8,128)S(1)}) custom-call(s32[16]{0:T(128)S(1)} %get-tuple-element.84.rows_ref, s32[16]{0:T(128)S(1)} %get-tuple-element.83.cols_ref, s32[16]{0:T(128)S(1)} %fusion.valid_ref, s32[2]{0:T(128)S(1)} %pad_add_fusion.at_ref, ...), custom_call_target="tpu_custom_call", output_to_operand_aliasing={{0}: (9, {})} | custom-call | flops 1000 | bytes 1000 | tf_op jit(solution)/shard_map/pallas_call | solution.py:185
  113.3 3.4 %shard_map.62 = (bf16[4,2,256,256]{3,2,1,0:T(8,128)(2,1)S(1)}, bf16[4,2,256,256]{3,2,1,0:T(8,128)(2,1)S(1)}, bf16[4,2,256,256]{3,2,1,0:T(8,128)(2,1)S(1)}, bf16[...) custom-call(s32[16]{0:T(128)S(1)} %get-tuple-element.82.rows_ref, ...), custom_call_target="tpu_custom_call" | custom-call | flops 1000 | bytes 1000 | tf_op jit(solution)/shard_map/pallas_call | solution.py:185
  116.8 0.5 collective-permute-start.21
  117.3 0.1 collective-permute-start.17
  117.4 4.5 %collective-permute-done.6.refs_0_ = bf16[2816,128]{1,0:T(8,128)(2,1)S(1)} collective-permute-done((bf16[2816,128]{1,0:T(8,128)(2,1)S(1)}, bf16[2816,128]{1,0:T(8,128)(2,1)S(1)}, u32[]{:S(2)}, u32[]{:S(2)}) %collective-permute-start.6) | collective-permute-done | bytes 720928 | tf_op jit(solution)/shard_map/ppermute | solution.py:211
  121.9 0.5 collective-permute-start.19
  122.5 0.4 collective-permute-start.16
  122.9 3.1 %shard_map.63 = (f32[16,2,256,256]{3,2,1,0:T(8,128)S(1)}, f32[8,128]{1,0:T(8,128)S(1)}) custom-call(s32[16]{0:T(128)S(1)} %get-tuple-element.84.rows_ref, s32[16]{0:T(128)S(1)} %get-tuple-element.83.cols_ref, s32[16]{0:T(128)S(1)} %fusion.valid_ref, s32[2]{0:T(128)S(1)} %pad_add_fusion.at_ref, ...), custom_call_target="tpu_custom_call", output_to_operand_aliasing={{0}: (7, {})} | custom-call | flops 1000 | bytes 1000 | tf_op jit(solution)/shard_map/pallas_call | solution.py:185
  126.1 1.0 collective-permute-done.15.refs_0_
  127.1 1.0 collective-permute-done.16.refs_1_
  128.1 4.4 %shard_map.64 = f32[16,2,256,256]{3,2,1,0:T(8,128)} custom-call(s32[16]{0:T(128)S(1)} %get-tuple-element.84.rows_ref, s32[16]{0:T(128)S(1)} %get-tuple-element.83.cols_ref, s32[16]{0:T(128)S(1)} %fusion.valid_ref, s32[2]{0:T(128)S(1)} %pad_add_fusion.at_ref, bf16[2816,128]{1,0:T(8,128)(2,1)S(1)} %collective-permute-done.15.refs_0_, ...), custom_call_target="tpu_custom_call" | custom-call | flops 1000 | bytes 1000 | tf_op jit(solution)/shard_map/pallas_call | solution.py:185
  (29 shorter events, 0.4 us)
Async XLA Ops:
  0.0 16.0 %copy-start.4 = (s32[256,2]{0,1:T(2,128)S(1)}, s32[256,2]{0,1:T(2,128)}, u32[]{:S(2)}) copy-start(s32[256,2]{0,1:T(2,128)} %param.8) | copy-start | bytes 6148
  2.8 7.1 %collective-permute-start.3 = (bf16[2816,128]{1,0:T(8,128)(2,1)}, bf16[2816,128]{1,0:T(8,128)(2,1)S(1)}, u32[]{:S(2)}, u32[]{:S(2)}) collective-permute-start(bf16[2816,128]{1,0:T(8,128)(2,1)} %get-tuple-element.42), channel_id=1, source_target_pairs={{0,1},{1,0},{2,3},{3,2},{4,5},{5,4},{6,7},{7,6},{8,9},{9,8},{10,11... | collective-permute-start | bytes 2162696 | tf_op jit(solution)/shard_map/ppermute | solution.py:214
  3.3 35.1 %collective-permute-start = (bf16[2816,128]{1,0:T(8,128)(2,1)}, bf16[2816,128]{1,0:T(8,128)(2,1)S(1)}, u32[]{:S(2)}, u32[]{:S(2)}) collective-permute-start(bf16[2816,128]{1,0:T(8,128)(2,1)} %get-tuple-element.41.refs_0_), channel_id=1, source_target_pairs={{0,4},{2,6},{4,0},{6,2},{8,12},{10,14},{12,8},{14,10},{1,5},{3,7},... | collective-permute-start | bytes 2162696 | tf_op jit(solution)/shard_map/ppermute | solution.py:211
  5.9 34.7 %collective-permute-start.1 = (bf16[2816,128]{1,0:T(8,128)(2,1)}, bf16[2816,128]{1,0:T(8,128)(2,1)S(1)}, u32[]{:S(2)}, u32[]{:S(2)}) collective-permute-start(bf16[2816,128]{1,0:T(8,128)(2,1)} %get-tuple-element.41.refs_0_), channel_id=1, source_target_pairs={{0,8},{2,10},{4,12},{6,14},{8,0},{10,2},{12,4},{14,6},{1,9},{3,11}... | collective-permute-start | bytes 2162696 | tf_op jit(solution)/shard_map/ppermute | solution.py:211
  8.5 32.1 %collective-permute-start.2 = (bf16[2816,128]{1,0:T(8,128)(2,1)}, bf16[2816,128]{1,0:T(8,128)(2,1)S(1)}, u32[]{:S(2)}, u32[]{:S(2)}) collective-permute-start(bf16[2816,128]{1,0:T(8,128)(2,1)} %get-tuple-element.41.refs_0_), channel_id=1, source_target_pairs={{0,2},{2,0},{4,6},{6,4},{8,10},{10,8},{12,14},{14,12},{1,3},{3,1},... | collective-permute-start | bytes 2162696 | tf_op jit(solution)/shard_map/ppermute | solution.py:211
  10.0 32.3 %collective-permute-start.4 = (bf16[2816,128]{1,0:T(8,128)(2,1)S(1)}, bf16[2816,128]{1,0:T(8,128)(2,1)}, u32[]{:S(2)}, u32[]{:S(2)}) collective-permute-start(bf16[2816,128]{1,0:T(8,128)(2,1)S(1)} %collective-permute-done.3.refs_1_), channel_id=1, source_target_pairs={{0,2},{2,0},{4,6},{6,4},{8,10},{10,8},{12,14},{14,12},{1,3},{3,1},... | collective-permute-start | bytes 2162696 | tf_op jit(solution)/shard_map/ppermute | solution.py:211
  10.5 1.2 copy-start.2
  11.7 0.7 copy-start.3
  16.2 52.1 %collective-permute-start.7 = (bf16[2816,128]{1,0:T(8,128)(2,1)S(1)}, bf16[2816,128]{1,0:T(8,128)(2,1)S(1)}, u32[]{:S(2)}, u32[]{:S(2)}) collective-permute-start(bf16[2816,128]{1,0:T(8,128)(2,1)S(1)} %collective-permute-done.3.refs_1_), channel_id=1, source_target_pairs={{0,4},{2,6},{4,0},{6,2},{8,12},{10,14},{12,8},{14,10},{1,5},{3,7},... | collective-permute-start | bytes 2162696 | tf_op jit(solution)/shard_map/ppermute | solution.py:211
  38.4 34.4 %collective-permute-start.8 = (bf16[2816,128]{1,0:T(8,128)(2,1)S(1)}, bf16[2816,128]{1,0:T(8,128)(2,1)S(1)}, u32[]{:S(2)}, u32[]{:S(2)}) collective-permute-start(bf16[2816,128]{1,0:T(8,128)(2,1)S(1)} %collective-permute-done.3.refs_1_), channel_id=1, source_target_pairs={{0,8},{2,10},{4,12},{6,14},{8,0},{10,2},{12,4},{14,6},{1,9},{3,11}... | collective-permute-start | bytes 2162696 | tf_op jit(solution)/shard_map/ppermute | solution.py:211
  42.2 30.6 %collective-permute-start.10 = (bf16[2816,128]{1,0:T(8,128)(2,1)S(1)}, bf16[2816,128]{1,0:T(8,128)(2,1)S(1)}, u32[]{:S(2)}, u32[]{:S(2)}) collective-permute-start(bf16[2816,128]{1,0:T(8,128)(2,1)S(1)} %collective-permute-done.1.refs_2_), channel_id=1, source_target_pairs={{0,2},{2,0},{4,6},{6,4},{8,10},{10,8},{12,14},{14,12},{1,3},{3,1},... | collective-permute-start | bytes 2162696 | tf_op jit(solution)/shard_map/ppermute | solution.py:211
  43.7 31.1 %collective-permute-start.9 = (bf16[2816,128]{1,0:T(8,128)(2,1)S(1)}, bf16[2816,128]{1,0:T(8,128)(2,1)S(1)}, u32[]{:S(2)}, u32[]{:S(2)}) collective-permute-start(bf16[2816,128]{1,0:T(8,128)(2,1)S(1)} %collective-permute-done.refs_0_), channel_id=1, source_target_pairs={{0,2},{2,0},{4,6},{6,4},{8,10},{10,8},{12,14},{14,12},{1,3},{3,1},... | collective-permute-start | bytes 2162696 | tf_op jit(solution)/shard_map/ppermute | solution.py:211
  44.3 40.5 %collective-permute-start.5 = (bf16[2816,128]{1,0:T(8,128)(2,1)S(1)}, bf16[2816,128]{1,0:T(8,128)(2,1)S(1)}, u32[]{:S(2)}, u32[]{:S(2)}) collective-permute-start(bf16[2816,128]{1,0:T(8,128)(2,1)S(1)} %collective-permute-done.1.refs_2_), channel_id=1, source_target_pairs={{0,4},{2,6},{4,0},{6,2},{8,12},{10,14},{12,8},{14,10},{1,5},{3,7},... | collective-permute-start | bytes 2162696 | tf_op jit(solution)/shard_map/ppermute | solution.py:211
  44.9 1.1 copy-start.1
  49.4 3.4 %copy-start = (f32[16,2,256,256]{3,2,1,0:T(8,128)S(1)}, f32[16,2,256,256]{3,2,1,0:T(8,128)}, u32[]{:S(2)}) copy-start(f32[16,2,256,256]{3,2,1,0:T(8,128)} %refs_5_.1) | copy-start | bytes 25165828
  74.8 19.1 %collective-permute-start.11 = (bf16[2816,128]{1,0:T(8,128)(2,1)S(1)}, bf16[2816,128]{1,0:T(8,128)(2,1)S(1)}, u32[]{:S(2)}, u32[]{:S(2)}) collective-permute-start(bf16[2816,128]{1,0:T(8,128)(2,1)S(1)} %collective-permute-done.8.refs_3_), channel_id=1, source_target_pairs={{0,2},{2,0},{4,6},{6,4},{8,10},{10,8},{12,14},{14,12},{1,3},{3,1},... | collective-permute-start | bytes 2162696 | tf_op jit(solution)/shard_map/ppermute | solution.py:211
  76.3 27.4 %collective-permute-start.13 = (bf16[2816,128]{1,0:T(8,128)(2,1)S(1)}, bf16[2816,128]{1,0:T(8,128)(2,1)S(1)}, u32[]{:S(2)}, u32[]{:S(2)}) collective-permute-start(bf16[2816,128]{1,0:T(8,128)(2,1)S(1)} %collective-permute-done.8.refs_3_), channel_id=1, source_target_pairs={{0,4},{2,6},{4,0},{6,2},{8,12},{10,14},{12,8},{14,10},{1,5},{3,7},... | collective-permute-start | bytes 2162696 | tf_op jit(solution)/shard_map/ppermute | solution.py:211
  76.7 32.6 %collective-permute-start.14 = (bf16[2816,128]{1,0:T(8,128)(2,1)S(1)}, bf16[2816,128]{1,0:T(8,128)(2,1)S(1)}, u32[]{:S(2)}, u32[]{:S(2)}) collective-permute-start(bf16[2816,128]{1,0:T(8,128)(2,1)S(1)} %collective-permute-done.7.refs_1_), channel_id=1, source_target_pairs={{0,2},{2,0},{4,6},{6,4},{8,10},{10,8},{12,14},{14,12},{1,3},{3,1},... | collective-permute-start | bytes 2162696 | tf_op jit(solution)/shard_map/ppermute | solution.py:211
  84.9 37.0 %collective-permute-start.6 = (bf16[2816,128]{1,0:T(8,128)(2,1)S(1)}, bf16[2816,128]{1,0:T(8,128)(2,1)S(1)}, u32[]{:S(2)}, u32[]{:S(2)}) collective-permute-start(bf16[2816,128]{1,0:T(8,128)(2,1)S(1)} %collective-permute-done.5.refs_0_), channel_id=1, source_target_pairs={{0,2},{2,0},{4,6},{6,4},{8,10},{10,8},{12,14},{14,12},{1,3},{3,1},... | collective-permute-start | bytes 2162696 | tf_op jit(solution)/shard_map/ppermute | solution.py:211
  93.9 28.0 %collective-permute-start.12 = (bf16[2816,128]{1,0:T(8,128)(2,1)S(1)}, bf16[2816,128]{1,0:T(8,128)(2,1)S(1)}, u32[]{:S(2)}, u32[]{:S(2)}) collective-permute-start(bf16[2816,128]{1,0:T(8,128)(2,1)S(1)} %collective-permute-done.11.refs_5_), channel_id=1, source_target_pairs={{0,4},{2,6},{4,0},{6,2},{8,12},{10,14},{12,8},{14,10},{1,5},{3,7},... | collective-permute-start | bytes 2162696 | tf_op jit(solution)/shard_map/ppermute | solution.py:211
  116.8 5.7 %collective-permute-start.20 = (bf16[2,2,256,256]{3,2,1,0:T(8,128)(2,1)S(1)}, bf16[2,2,256,256]{3,2,1,0:T(8,128)(2,1)S(1)}, u32[]{:S(2)}, u32[]{:S(2)}) collective-permute-start(bf16[2,2,256,256]{3,2,1,0:T(8,128)(2,1)S(1)} %get-tuple-element.74), channel_id=1, source_target_pairs={{0,1},{1,0},{2,3},{3,2},{4,5},{5,4},{6,7},{7,6},{8,9},{9,8},{10,11... | collective-permute-start | bytes 1572872 | tf_op jit(solution)/shard_map/ppermute | solution.py:214
  116.8 5.7 %collective-permute-start.21 = (bf16[2,2,256,256]{3,2,1,0:T(8,128)(2,1)S(1)}, bf16[2,2,256,256]{3,2,1,0:T(8,128)(2,1)S(1)}, u32[]{:S(2)}, u32[]{:S(2)}) collective-permute-start(bf16[2,2,256,256]{3,2,1,0:T(8,128)(2,1)S(1)} %get-tuple-element.75), channel_id=1, source_target_pairs={{0,1},{1,0},{2,3},{3,2},{4,5},{5,4},{6,7},{7,6},{8,9},{9,8},{10,11... | collective-permute-start | bytes 1572872 | tf_op jit(solution)/shard_map/ppermute | solution.py:214
  117.3 8.7 %collective-permute-start.17 = (bf16[4,2,256,256]{3,2,1,0:T(8,128)(2,1)S(1)}, bf16[4,2,256,256]{3,2,1,0:T(8,128)(2,1)S(1)}, u32[]{:S(2)}, u32[]{:S(2)}) collective-permute-start(bf16[4,2,256,256]{3,2,1,0:T(8,128)(2,1)S(1)} %get-tuple-element.71), channel_id=1, source_target_pairs={{0,1},{1,0},{2,3},{3,2},{4,5},{5,4},{6,7},{7,6},{8,9},{9,8},{10,11... | collective-permute-start | bytes 3145736 | tf_op jit(solution)/shard_map/ppermute | solution.py:214
  121.9 4.1 %collective-permute-start.18 = (bf16[4,2,256,256]{3,2,1,0:T(8,128)(2,1)S(1)}, bf16[4,2,256,256]{3,2,1,0:T(8,128)(2,1)S(1)}, u32[]{:S(2)}, u32[]{:S(2)}) collective-permute-start(bf16[4,2,256,256]{3,2,1,0:T(8,128)(2,1)S(1)} %get-tuple-element.72), channel_id=1, source_target_pairs={{0,1},{1,0},{2,3},{3,2},{4,5},{5,4},{6,7},{7,6},{8,9},{9,8},{10,11... | collective-permute-start | bytes 3145736 | tf_op jit(solution)/shard_map/ppermute | solution.py:214
  121.9 4.2 %collective-permute-start.19 = (bf16[4,2,256,256]{3,2,1,0:T(8,128)(2,1)S(1)}, bf16[4,2,256,256]{3,2,1,0:T(8,128)(2,1)S(1)}, u32[]{:S(2)}, u32[]{:S(2)}) collective-permute-start(bf16[4,2,256,256]{3,2,1,0:T(8,128)(2,1)S(1)} %get-tuple-element.73), channel_id=1, source_target_pairs={{0,1},{1,0},{2,3},{3,2},{4,5},{5,4},{6,7},{7,6},{8,9},{9,8},{10,11... | collective-permute-start | bytes 3145736 | tf_op jit(solution)/shard_map/ppermute | solution.py:214
  122.4 4.7 %collective-permute-start.15 = (bf16[2816,128]{1,0:T(8,128)(2,1)S(1)}, bf16[2816,128]{1,0:T(8,128)(2,1)S(1)}, u32[]{:S(2)}, u32[]{:S(2)}) collective-permute-start(bf16[2816,128]{1,0:T(8,128)(2,1)S(1)} %collective-permute-done.12.refs_1_), channel_id=1, source_target_pairs={{0,1},{1,0},{2,3},{3,2},{4,5},{5,4},{6,7},{7,6},{8,9},{9,8},{10,11... | collective-permute-start | bytes 2162696 | tf_op jit(solution)/shard_map/ppermute | solution.py:214
  122.5 5.6 %collective-permute-start.16 = (bf16[2816,128]{1,0:T(8,128)(2,1)S(1)}, bf16[2816,128]{1,0:T(8,128)(2,1)S(1)}, u32[]{:S(2)}, u32[]{:S(2)}) collective-permute-start(bf16[2816,128]{1,0:T(8,128)(2,1)S(1)} %collective-permute-done.6.refs_0_), channel_id=1, source_target_pairs={{0,1},{1,0},{2,3},{3,2},{4,5},{5,4},{6,7},{7,6},{8,9},{9,8},{10,11... | collective-permute-start | bytes 2162696 | tf_op jit(solution)/shard_map/ppermute | solution.py:214
